TPU v7x, 256 devices: a whole 4x4x8 slice. The times are simulated.
256 devices in a mesh: dp: 16 (over x, z_hi), tensor: 16 (over y, z_lo, core).
Axes of the slice: x: 4, y: 4, z: 8 (z_hi: 4, z_lo: 2; z = z_hi * 2 + z_lo), core: 2. Of those that a mesh axis runs over, the one named last changes fastest.
Arguments:
- acts: bfloat16 [2048, 4096], P('dp', 'tensor'), may hold values from -6 to 6
- grads: bfloat16 [2048, 14336], P('dp', 'tensor'), may hold values from -6 to 6
- basis_in: bfloat16 [4096, 4096], P(None, 'tensor'), may hold values from -0.09375 to 0.09375
- basis_out: bfloat16 [14336, 14336], P('tensor', 'dp'), may hold values from -0.046875 to 0.046875
- scale_old: float32 [4096, 14336], P('tensor', 'dp'), may hold values from 0.25 to 4
Outputs:
- scale_new: float32 [4096, 14336], P('tensor', 'dp')
- step: bfloat16 [4096, 14336], P('dp', 'tensor')
All inputs are finite; a program needn't handle non-finite values.
Results may differ from a plain program's by a relative error of at most 0.029.
Values may be sent and summed in bfloat16 or wider, within the bound.
No kernel may reach another device: no remote copies, remote signals or barrier semaphores. Data moves between devices by JAX's collectives and lax.ppermute only.
A program may use at most 64 MiB of HBM per device.

v0:
```python
import math

import jax
import jax.numpy as jnp
from jax import lax
from jax.sharding import PartitionSpec as P

decay_rate = 0.5
damping = 0.1


def body(acts, grads, basis_in, basis_out, scale_old):
    selected = basis_in
    act_local = jnp.dot(
        lax.all_gather(acts, "tensor", axis=1, tiled=True),
        selected,
        preferred_element_type=jnp.float32,
    ).astype(jnp.bfloat16)
    act_proj = lax.all_gather(act_local, "dp", axis=0, tiled=True)
    grad_all = lax.all_gather(grads, "dp", axis=0, tiled=True)
    tokens_total = grad_all.shape[0]
    selected = grad_all
    grad_share = lax.psum_scatter(
        jnp.dot(selected, basis_out, preferred_element_type=jnp.float32).astype(jnp.bfloat16),
        "tensor",
        scatter_dimension=0,
        tiled=True,
    )
    grad_proj = lax.all_gather(grad_share, "tensor", axis=0, tiled=True)
    act_square = act_proj * act_proj
    grad_square = grad_proj * grad_proj
    contract = (((0,), (0,)), ((), ()))
    window = (
        lax.dot_general(act_square, grad_square, contract, preferred_element_type=jnp.float32)
        / tokens_total
    )
    mean_grad = (
        lax.dot_general(act_proj, grad_proj, contract, preferred_element_type=jnp.float32)
        / tokens_total
    )
    scale_new = decay_rate * scale_old + (1.0 - decay_rate) * window
    corrected = (mean_grad / (scale_new + damping)).astype(jnp.bfloat16)
    partial_value = jnp.dot(basis_in, corrected, preferred_element_type=jnp.float32)
    left = lax.psum(partial_value.astype(jnp.bfloat16), "tensor")
    selected = left
    update_share = lax.psum_scatter(
        lax.dot_general(
            selected, basis_out, (((1,), (1,)), ((), ())), preferred_element_type=jnp.float32
        ).astype(jnp.bfloat16),
        "dp",
        scatter_dimension=0,
        tiled=True,
    ).astype(jnp.float32)
    step = (-math.sqrt(tokens_total) * update_share).astype(jnp.bfloat16)
    return (scale_new, step)


def solution(mesh):
    return jax.shard_map(
        body,
        mesh=mesh,
        in_specs=(
            P("dp", "tensor"),
            P("dp", "tensor"),
            P(None, "tensor"),
            P("tensor", "dp"),
            P("tensor", "dp"),
        ),
        out_specs=(P("tensor", "dp"), P("dp", "tensor")),
        check_vma=False,
    )
```

profile of v0, /device:TPU:1, one launch (start us, length us, event | category | flops | bytes accessed | tf_op | source)
XLA Modules:
  0.0 615.4 jit_solution(2876048984355306868)
XLA Ops:
  7.2 0.0 copy-start
  7.2 0.0 all-gather.9.cloned.1.call-start
  7.2 0.7 all-gather.9.cloned.1.call-update
  7.9 0.0 all-gather.5.cloned.1.call-start
  8.0 0.7 all-gather.5.cloned.1.call-update
  8.7 0.0 reduce-scatter.3.cloned.1.call-start
  8.7 77.2 %all-gather.9.cloned.1.call-done = bf16[2048,896]{1,0:T(8,128)(2,1)} async-done(((bf16[128,896]{1,0:T(8,128)(2,1)}), bf16[2048,896]{1,0:T(8,128)(2,1)}) %all-gather.9.cloned.1.call-update) | async-done | bytes 3670032 | tf_op jit(solution)/shard_map/all_gather | solution.py:20
  85.9 8.7 %convolution_convert_fusion.1 = bf16[2048,896]{1,0:T(8,128)(2,1)} fusion(bf16[2048,896]{1,0:T(8,128)(2,1)} %all-gather.9.cloned.1.call-done, bf16[896,896]{1,0:T(8,128)(2,1)} %param.8), kind=kOutput, calls=%fused_computation.4 | convolution fusion | flops 3290169344 | bytes 8945664 | tf_op jit(solution)/shard_map/dot_general | solution.py:24
  94.6 0.0 reduce-scatter.3.cloned.1.call-update
  94.6 0.0 all-gather.7.cloned.1.call-start
  94.7 28.9 %all-gather.5.cloned.1.call-done = bf16[128,4096]{1,0:T(8,128)(2,1)} async-done(((bf16[128,256]{1,0:T(8,128)(2,1)}), bf16[128,4096]{1,0:T(8,128)(2,1)}) %all-gather.5.cloned.1.call-update) | async-done | bytes 1048592 | tf_op jit(solution)/shard_map/all_gather | solution.py:15
  123.6 0.0 copy-done
  123.6 2.3 convolution_convert_fusion.2
  125.9 0.0 all-gather.7.cloned.1.call-update
  125.9 0.0 all-gather.11.cloned.1.call-start
  125.9 67.9 %reduce-scatter.3.cloned.1.call-done = bf16[128,896]{1,0:T(8,128)(2,1)} async-done(((bf16[2048,896]{1,0:T(8,128)(2,1)}), bf16[128,896]{1,0:T(8,128)(2,1)}) %reduce-scatter.3.cloned.1.call-update) | async-done | bytes 229392 | tf_op jit(solution)/shard_map/reduce_scatter | solution.py:23
  193.9 0.0 all-gather.11.cloned.1.call-update
  193.9 0.0 all-reduce.2.cloned.1.call-start
  193.9 55.8 %all-gather.7.cloned.1.call-done = bf16[2048,256]{1,0:T(8,128)(2,1)} async-done(((bf16[128,256]{1,0:T(8,128)(2,1)}), bf16[2048,256]{1,0:T(8,128)(2,1)}) %all-gather.7.cloned.1.call-update) | async-done | bytes 1048592 | tf_op jit(solution)/shard_map/all_gather | solution.py:19
  249.7 0.0 copy-start.1
  249.7 39.9 %all-gather.11.cloned.1.call-done = bf16[2048,896]{1,0:T(8,128)(2,1)} async-done(((bf16[128,896]{1,0:T(8,128)(2,1)}), bf16[2048,896]{1,0:T(8,128)(2,1)}) %all-gather.11.cloned.1.call-update) | async-done | bytes 3670032 | tf_op jit(solution)/shard_map/all_gather | solution.py:29
  289.7 4.8 fusion.5
  294.5 0.0 copy-done.1
  294.5 9.0 %convert_bitcast_fusion = bf16[4096,896]{0,1:T(8,128)(2,1)} fusion(bf16[4096,256]{1,0:T(8,128)(2,1)S(1)} %copy-done, bf16[2048,256]{1,0:T(8,128)(2,1)S(1)} %copy-done.1, bf16[2048,896]{1,0:T(8,128)(2,1)} %all-gather.11.cloned.1.call-done, f32[256,896]{1,0:T(8,128)} %fusion.5), kind=kOutput, calls=%fused_computation | convolution fusion | flops 2823159808 | bytes 15073280 | tf_op jit(solution)/shard_map/dot_general | solution.py:43
  303.5 0.0 all-reduce.2.cloned.1.call-update
  303.5 0.2 reduce-scatter.5.cloned.1.call-start
  303.7 176.6 %all-reduce.2.cloned.1.call-done = bf16[4096,896]{0,1:T(8,128)(2,1)} async-done(((bf16[4096,896]{0,1:T(8,128)(2,1)}), bf16[4096,896]{0,1:T(8,128)(2,1)}) %all-reduce.2.cloned.1.call-update) | async-done | bytes 7340048 | tf_op jit(solution)/shard_map/psum | solution.py:44
  480.4 13.4 %convolution_convert_fusion = bf16[4096,896]{1,0:T(8,128)(2,1)} fusion(bf16[4096,896]{0,1:T(8,128)(2,1)} %all-reduce.2.cloned.1.call-done, bf16[896,896]{1,0:T(8,128)(2,1)} %param.8), kind=kOutput, calls=%fused_computation.1 | convolution fusion | flops 6580338688 | bytes 16285696 | tf_op jit(solution)/shard_map/dot_general | solution.py:47
  493.7 0.0 reduce-scatter.5.cloned.1.call-update
  493.7 113.0 %reduce-scatter.5.cloned.1.call-done = bf16[256,896]{1,0:T(8,128)(2,1)} async-done(((bf16[4096,896]{1,0:T(8,128)(2,1)}), bf16[256,896]{1,0:T(8,128)(2,1)}) %reduce-scatter.5.cloned.1.call-update) | async-done | bytes 458768 | tf_op jit(solution)/shard_map/reduce_scatter | solution.py:46
  606.7 1.9 multiply_convert_fusion
Async XLA Ops:
  7.2 116.4 %copy-start = (bf16[4096,256]{1,0:T(8,128)(2,1)S(1)}, bf16[4096,256]{1,0:T(8,128)(2,1)}, u32[]{:S(2)}) copy-start(bf16[4096,256]{1,0:T(8,128)(2,1)} %param.7) | copy-start | bytes 6291460
  7.2 78.7 %all-gather.9.cloned.1.call-start = ((), (), s32[]{:S(2)}) async-start(), calls=%async_computation.4 | async-start | bytes 3899392 | tf_op jit(solution)/shard_map/all_gather | solution.py:20
  7.9 115.6 %all-gather.5.cloned.1.call-start = ((), (), s32[]{:S(2)}) async-start(), calls=%async_computation.2 | async-start | bytes 1114112 | tf_op jit(solution)/shard_map/all_gather | solution.py:15
  8.7 185.2 %reduce-scatter.3.cloned.1.call-start = ((), (), s32[]{:S(2)}) async-start(), calls=%async_computation.5 | async-start | bytes 3899392 | tf_op jit(solution)/shard_map/reduce_scatter | solution.py:23
  94.6 155.1 %all-gather.7.cloned.1.call-start = ((), (), s32[]{:S(2)}) async-start(), calls=%async_computation.3 | async-start | bytes 1114112 | tf_op jit(solution)/shard_map/all_gather | solution.py:19
  125.9 163.8 %all-gather.11.cloned.1.call-start = ((), (), s32[]{:S(2)}) async-start(), calls=%async_computation.6 | async-start | bytes 3899392 | tf_op jit(solution)/shard_map/all_gather | solution.py:29
  193.9 286.5 %all-reduce.2.cloned.1.call-start = ((), (), s32[]{:S(2)}) async-start(), calls=%async_computation.7 | async-start | bytes 14680064 | tf_op jit(solution)/shard_map/psum | solution.py:44
  249.7 44.8 %copy-start.1 = (bf16[2048,256]{1,0:T(8,128)(2,1)S(1)}, bf16[2048,256]{1,0:T(8,128)(2,1)}, u32[]{:S(2)}) copy-start(bf16[2048,256]{1,0:T(8,128)(2,1)} %all-gather.7.cloned.1.call-done) | copy-start | bytes 3145732
  303.5 303.2 %reduce-scatter.5.cloned.1.call-start = ((), (), s32[]{:S(2)}) async-start(), calls=%async_computation.8 | async-start | bytes 7798784 | tf_op jit(solution)/shard_map/reduce_scatter | solution.py:46
Sparse Core Ops, SparseCore 0:
  10.5 75.3 all-gather.8
  87.7 35.8 all-gather.4
  126.1 67.7 reduce-scatter.2
  196.7 52.9 all-gather.6
  251.4 38.1 all-gather.10
  303.6 176.6 all-reduce.1
  493.9 112.8 reduce-scatter.4
where the time goes:
time: 616 us; the launch traced here: 615 us
  waiting for transfers between devices  561 us (91%)
  matrix products  38.2 us (6%)
  between operations  14.1 us (2%)
    psum x1, waiting for transfers between devices, body(): left = lax.psum(partial_value.astype(jnp.bfloat16), 'tensor')  177 us
    reduce_scatter x1, waiting for transfers between devices, body(): lax.psum_scatter(lax.dot_general(selected, basis_out, (((1,), (1,)), ((),...  113 us
    all_gather x1, waiting for transfers between devices, body(): grad_all = lax.all_gather(grads, 'dp', axis=0, tiled=True)  77.2 us
    reduce_scatter x1, waiting for transfers between devices, body(): lax.psum_scatter(jnp.dot(selected, basis_out, preferred_element_type=jnp....  67.9 us
    all_gather x1, waiting for transfers between devices, body(): act_proj = lax.all_gather(act_local, 'dp', axis=0, tiled=True)  55.8 us
    all_gather x1, waiting for transfers between devices, body(): grad_proj = lax.all_gather(grad_share, 'tensor', axis=0, tiled=True)  39.9 us
    all_gather x1, waiting for transfers between devices, body(): lax.all_gather(acts, 'tensor', axis=1, tiled=True)  28.9 us
    dot_general x1, matrix products, body(): lax.dot_general(selected, basis_out, (((1,), (1,)), ((), ())), preferred_...  13.4 us
  transfers between devices with their start and end apart: 7, of which 7 were waited for; matrix products, arithmetic and copies ran while one was open for 2% of the time, Pallas kernels for 0%

commit v1 on v0

v1 whole, which is shorter than its diff:
```python
import math

import jax
import jax.numpy as jnp
from jax import lax
from jax.sharding import Mesh, PartitionSpec as P

decay_rate = 0.5
damping = 0.1
SIZES = {"x": 4, "zh": 4, "y": 4, "zl": 2, "c": 2}
TOKEN_CHUNKS = 2
WIDTHS = (64, 64)
bf16 = jnp.bfloat16


def swap(value):
    return lax.ppermute(value, "c", [(0, 1), (1, 0)])


def after(value, token):
    return lax.optimization_barrier((value, token))[0]


def roll(value, shift, axis):
    return lax.dynamic_slice_in_dim(
        jnp.concatenate([value, value], axis), shift % value.shape[axis], value.shape[axis], axis
    )


def dot(a, b, dims=((1,), (0,))):
    return lax.dot_general(a, b, (dims, ((), ())), preferred_element_type=jnp.float32)


def count(axes):
    return math.prod(SIZES[axis] for axis in axes)


def gather(value, axes):
    copies = jnp.broadcast_to(value[None], (count(axes),) + value.shape)
    return lax.all_to_all(copies, axes, 0, 0, tiled=True)


def reduce(value, axes):
    got = lax.all_to_all(value, axes, 0, 0, tiled=True)
    got = got.reshape((count(axes), -1) + value.shape[1:])
    return jnp.sum(got.astype(jnp.float32), 0).astype(bf16)


def body(acts, grads, basis_in, basis_out, scale_old):
    c = lax.axis_index("c")
    around = ("y", "zl")

    halves = roll(grads.reshape(2, 64, 896), c, 0)
    grads_chip = jnp.concatenate([halves[0], swap(halves[1])], 1)
    out_chip = jnp.concatenate([basis_out, swap(basis_out)], 0)

    width = 64 // TOKEN_CHUNKS
    lines = [
        lax.all_gather(grads_chip[m * width : (m + 1) * width], ("x", "zh"), axis=0, tiled=True)
        for m in range(TOKEN_CHUNKS)
    ]

    features = gather(acts, ("y", "zl", "c"))
    act_local = dot(features, basis_in.reshape(16, 256, 256), ((0, 2), (0, 1))).astype(bf16)
    act_local = roll(act_local.reshape(2, 64, 256), c, 0).reshape(2, TOKEN_CHUNKS, width, 256)
    act_proj = gather(gather(act_local, ("zh",)), ("x",))
    act_proj = jnp.transpose(act_proj, (2, 3, 0, 1, 4, 5)).reshape(2048, 256)
    out_chip = after(out_chip, act_proj)

    own, other = [], []
    for line in lines:
        term = dot(line, out_chip).astype(bf16)
        own.append(gather(reduce(term, around), around).reshape(-1, 896))
        other.append(swap(own[-1]))
    grad_proj = jnp.concatenate(own + other, 0)

    act_square = act_proj * act_proj
    grad_square = grad_proj * grad_proj
    window = dot(act_square, grad_square, ((0,), (0,))) / 2048
    mean_grad = dot(act_proj, grad_proj, ((0,), (0,))) / 2048
    scale_new = decay_rate * scale_old + (1.0 - decay_rate) * window
    corrected = (mean_grad / (scale_new + damping)).astype(bf16)
    corrected_chip = jnp.concatenate([corrected, swap(corrected)], 0)

    by_core = roll(basis_in.reshape(16, 2, 128, 256), c, 1)
    in_chip = jnp.concatenate([by_core[:, 0], swap(by_core[:, 1])], 2)

    steps = []
    begin = 0
    for width in WIDTHS:
        rows = in_chip[:, begin : begin + width].reshape(16 * width, 512)
        begin += width
        piece = reduce(dot(rows, corrected_chip).astype(bf16), around)
        left = gather(piece, around).reshape(16 * width, 896)
        update = dot(left, out_chip, ((1,), (1,))).astype(bf16)
        steps.append(lax.psum_scatter(update, ("x", "zh"), scatter_dimension=0, tiled=True))
    step = (-math.sqrt(2048) * jnp.concatenate(steps, 0).astype(jnp.float32)).astype(bf16)
    both = jnp.stack([step[:, :896], swap(step[:, 896:])])
    return (scale_new, roll(both, c, 0).reshape(256, 896))


def solution(mesh):
    inner = Mesh(mesh.devices.reshape(4, 4, 4, 2, 2), ("x", "zh", "y", "zl", "c"))
    dp, tensor = ("x", "zh"), ("y", "zl", "c")
    return jax.shard_map(
        body,
        mesh=inner,
        in_specs=(P(dp, tensor), P(dp, tensor), P(None, tensor), P(tensor, dp), P(tensor, dp)),
        out_specs=(P(tensor, dp), P(dp, tensor)),
        check_vma=False,
    )
```

time: 616 us -> 466 us (0.76)
  waiting for transfers between devices: 561 us -> 220 us
  blocking collectives: 0 us -> 143 us
  starting transfers between devices: 0.46 us -> 38.6 us
  other arithmetic: 1.86 us -> 11 us
  local copies, waits for them, and re-layouts: 0.01 us -> 8.11 us
  matrix products: 38.2 us -> 30.6 us
    psum x1 -> x0, waiting for transfers between devices: 177 us -> none  [body(): left = lax.psum(partial_value.astype(jnp.bfloat16), 'tensor')]
    all_gather x4 -> x2, waiting for transfers between devices: 202 us -> 45.8 us  [body(): lax.all_gather(grads_chip[m * width:(m + 1) * width], ('x', 'zh'), axis=0...]
    all_to_all x0 -> x5, blocking collectives: none -> 143 us  [the longest x3 79.3 us: gather(): return lax.all_to_all(copies, axes, 0, 0, tiled=True)]
    reduce_scatter x2, waiting for transfers between devices: 181 us -> 108 us  [body(): lax.psum_scatter(update, ('x', 'zh'), scatter_dimension=0, tiled=True)]
    all_to_all x0 -> x6, waiting for transfers between devices: none -> 61.2 us  [the longest x4 48.4 us: gather(): return lax.all_to_all(copies, axes, 0, 0, tiled=True)]
    all_to_all x0 -> x6, starting transfers between devices: none -> 25.5 us  [the longest x4 16.6 us: gather(): return lax.all_to_all(copies, axes, 0, 0, tiled=True)]
    ppermute x0 -> x7, starting transfers between devices: none -> 12.9 us  [swap(): return lax.ppermute(value, 'c', [(0, 1), (1, 0)])]
    concatenate x0 -> x7, other arithmetic: none -> 7.9 us  [the longest x1 3.91 us: body(): out_chip = jnp.concatenate([basis_out, swap(basis_out)], 0)]
  transfers between devices with their start and end apart: 7 -> 17, of which waited for: 7 -> 12; matrix products, arithmetic and copies ran while one was open for 2% -> 8% of each run, Pallas kernels for 0% -> 0%
where the time goes in v1:
time: 466 us; the launch traced here: 465 us
  waiting for transfers between devices  220 us (47%)
  blocking collectives  143 us (31%)
  starting transfers between devices  38.6 us (8%)
  matrix products  30.6 us (7%)
  between operations  14 us (3%)
  other arithmetic  11 us (2%)
  local copies, waits for them, and re-layouts  8.11 us (2%)
    reduce_scatter x2, waiting for transfers between devices, body(): lax.psum_scatter(update, ('x', 'zh'), scatter_dimension=0, tiled=True)  108 us
    all_to_all x3, blocking collectives, gather(): return lax.all_to_all(copies, axes, 0, 0, tiled=True)  79.3 us
    all_to_all x2, blocking collectives, reduce(): got = lax.all_to_all(value, axes, 0, 0, tiled=True)  63.7 us
    all_to_all x4, waiting for transfers between devices, gather(): return lax.all_to_all(copies, axes, 0, 0, tiled=True)  48.4 us
    all_gather x2, waiting for transfers between devices, body(): lax.all_gather(grads_chip[m * width:(m + 1) * width], ('x', 'zh'), axis=0...  45.8 us
    dot_general x9, matrix products, dot(): lax.dot_general(a, b, (dims, ((), ())), preferred_element_type=jnp.float32)  30.6 us
    all_to_all x4, starting transfers between devices, gather(): return lax.all_to_all(copies, axes, 0, 0, tiled=True)  16.6 us
    ppermute x7, starting transfers between devices, swap(): return lax.ppermute(value, 'c', [(0, 1), (1, 0)])  12.9 us
  transfers between devices with their start and end apart: 17, of which 12 were waited for; matrix products, arithmetic and copies ran while one was open for 8% of the time, Pallas kernels for 0%

profile of v1, /device:TPU:1, one launch (start us, length us, event | category | flops | bytes accessed | tf_op | source)
XLA Modules:
  0.0 465.2 jit_solution(7662553360222844698)
XLA Ops:
  8.5 3.3 collective-permute-start
  13.5 1.9 broadcast_in_dim.16
  15.4 4.5 all-to-all-start
  20.6 16.3 %all-to-all-done = bf16[16,128,256]{2,1,0:T(8,128)(2,1)S(1)} async-done(((bf16[16,128,256]{2,1,0:T(8,128)(2,1)}), bf16[16,128,256]{2,1,0:T(8,128)(2,1)S(1)}, u32[]{:S(2)}, u32[]{:S(2)}) %all-to-all-start) | async-done | bytes 1048608 | tf_op jit(solution)/shard_map/all_to_all | solution.py:40
  37.4 17.6 %all_to_all.71 = bf16[4,2,2,32,256]{4,3,2,1,0:T(8,128)(2,1)S(1)} all-to-all(bf16[4,2,2,32,256]{4,3,2,1,0:T(8,128)(2,1)S(1)} %broadcast_in_dim.18), channel_id=1, replica_groups=mesh['x'=4,'zh'=4,'y'=4,'zl'=2,'c'=2] {'zh'}, dimensions={0} | all-to-all | bytes 524288 | tf_op jit(solution)/shard_map/all_to_all | solution.py:40
  56.2 4.2 all-to-all-start.2
  60.4 3.9 pad_maximum_fusion.1
  64.3 13.0 %all-to-all-done.2 = bf16[4,4,2,2,32,256]{5,4,1,3,2,0:T(8,128)(2,1)S(1)} async-done(((bf16[4,4,2,2,32,256]{5,4,1,3,2,0:T(8,128)(2,1)}), bf16[4,4,2,2,32,256]{5,4,1,3,2,0:T(8,128)(2,1)S(1)}, u32[]{:S(2)}, u32[]{:S(2)}) %all-to-all-start.2) | async-done | bytes 1048608 | tf_op jit(solution)/shard_map/all_to_all | solution.py:40
  78.4 5.5 %convolution_convert_fusion.5 = bf16[512,896]{1,0:T(8,128)(2,1)} fusion(bf16[512,1792]{1,0:T(8,128)(2,1)} %all-gather.3.cloned.1.call-done, bf16[1792,896]{1,0:T(8,128)(2,1)} %pad_maximum_fusion.1), kind=kOutput, calls=%fused_computation.14 | convolution fusion | flops 1644625920 | bytes 5963776 | tf_op jit(solution)/shard_map/dot_general | solution.py:31
  83.9 3.6 all-to-all-start.3
  87.5 45.8 %all-gather.5.cloned.1.call-done = bf16[512,1792]{1,0:T(8,128)(2,1)} async-done(((bf16[32,1792]{1,0:T(8,128)(2,1)}), bf16[512,1792]{1,0:T(8,128)(2,1)}) %all-gather.5.cloned.1.call-update) | async-done | bytes 1835024 | tf_op jit(solution)/shard_map/all_gather | solution.py:59
  133.3 5.4 %convolution_convert_fusion.4 = bf16[512,896]{1,0:T(8,128)(2,1)} fusion(bf16[512,1792]{1,0:T(8,128)(2,1)} %all-gather.5.cloned.1.call-done, bf16[1792,896]{1,0:T(8,128)(2,1)} %pad_maximum_fusion.1), kind=kOutput, calls=%fused_computation.13 | convolution fusion | flops 1644625920 | bytes 5963776 | tf_op jit(solution)/shard_map/dot_general | solution.py:31
  138.7 5.3 %all-to-all-start.5 = ((bf16[8,64,896]{2,1,0:T(8,128)(2,1)}), bf16[8,64,896]{2,1,0:T(8,128)(2,1)}, u32[]{:S(2)}, u32[]{:S(2)}) async-start(bf16[8,64,896]{2,1,0:T(8,128)(2,1)} %bitcast.62), calls=%async_computation.5 | async-start | bytes 1835008 | tf_op jit(solution)/shard_map/all_to_all | solution.py:44
  144.2 12.8 %all-to-all-done.5 = bf16[8,64,896]{2,1,0:T(8,128)(2,1)} async-done(((bf16[8,64,896]{2,1,0:T(8,128)(2,1)}), bf16[8,64,896]{2,1,0:T(8,128)(2,1)}, u32[]{:S(2)}, u32[]{:S(2)}) %all-to-all-start.5) | async-done | bytes 917536 | tf_op jit(solution)/shard_map/all_to_all | solution.py:44
  158.0 3.8 all-to-all-start.4
  161.7 1.3 reduce_sum.49
  163.1 10.9 %all-to-all-done.4 = bf16[8,64,896]{2,1,0:T(8,128)(2,1)S(1)} async-done(((bf16[8,64,896]{2,1,0:T(8,128)(2,1)}), bf16[8,64,896]{2,1,0:T(8,128)(2,1)S(1)}, u32[]{:S(2)}, u32[]{:S(2)}) %all-to-all-start.4) | async-done | bytes 917536 | tf_op jit(solution)/shard_map/all_to_all | solution.py:40
  175.0 4.2 all-to-all-start.6
  179.3 3.1 collective-permute-start.2
  182.5 8.2 %all-to-all-done.6 = bf16[8,64,896]{2,1,0:T(8,128)(2,1)} async-done(((bf16[8,64,896]{2,1,0:T(8,128)(2,1)}), bf16[8,64,896]{2,1,0:T(8,128)(2,1)}, u32[]{:S(2)}, u32[]{:S(2)}) %all-to-all-start.6) | async-done | bytes 917536 | tf_op jit(solution)/shard_map/all_to_all | solution.py:40
  190.6 4.0 collective-permute-start.3
  196.9 2.8 fusion.6
  199.7 3.1 fusion.10
  206.2 26.3 %all_to_all.72 = bf16[8,128,896]{2,1,0:T(8,128)(2,1)S(1)} all-to-all(bf16[8,128,896]{2,1,0:T(8,128)(2,1)S(1)} %bitcast.53), channel_id=1, replica_groups=mesh['x'=4,'zh'=4,'y'=4,'zl'=2,'c'=2] {'y','zl'}, dimensions={0} | all-to-all | bytes 3670016 | tf_op jit(solution)/shard_map/all_to_all | solution.py:44
  233.0 25.4 %all_to_all.73 = bf16[8,128,896]{2,1,0:T(8,128)(2,1)S(1)} all-to-all(bf16[8,128,896]{2,1,0:T(8,128)(2,1)S(1)} %broadcast_in_dim.22), channel_id=1, replica_groups=mesh['x'=4,'zh'=4,'y'=4,'zl'=2,'c'=2] {'y','zl'}, dimensions={0} | all-to-all | bytes 3670016 | tf_op jit(solution)/shard_map/all_to_all | solution.py:40
  258.4 5.4 %convolution_convert_fusion.1 = bf16[1024,1792]{1,0:T(8,128)(2,1)} fusion(bf16[1024,896]{1,0:T(8,128)(2,1)S(1)} %bitcast.54, bf16[1792,896]{1,0:T(8,128)(2,1)S(1)} %copy-done.1), kind=kOutput, calls=%fused_computation.3 | convolution fusion | flops 3290169344 | bytes 8716288 | tf_op jit(solution)/shard_map/dot_general | solution.py:31
  266.2 37.4 %all_to_all.74 = bf16[8,128,896]{2,1,0:T(8,128)(2,1)S(1)} all-to-all(bf16[8,128,896]{2,1,0:T(8,128)(2,1)S(1)} %bitcast.51), channel_id=1, replica_groups=mesh['x'=4,'zh'=4,'y'=4,'zl'=2,'c'=2] {'y','zl'}, dimensions={0} | all-to-all | bytes 3670016 | tf_op jit(solution)/shard_map/all_to_all | solution.py:44
  304.2 36.3 %all_to_all.75 = bf16[8,128,896]{2,1,0:T(8,128)(2,1)S(1)} all-to-all(bf16[8,128,896]{2,1,0:T(8,128)(2,1)S(1)} %broadcast_in_dim.23), channel_id=1, replica_groups=mesh['x'=4,'zh'=4,'y'=4,'zl'=2,'c'=2] {'y','zl'}, dimensions={0} | all-to-all | bytes 3670016 | tf_op jit(solution)/shard_map/all_to_all | solution.py:40
  340.5 5.5 %convolution_convert_fusion = bf16[1024,1792]{1,0:T(8,128)(2,1)} fusion(bf16[1024,896]{1,0:T(8,128)(2,1)S(1)} %bitcast.52, bf16[1792,896]{1,0:T(8,128)(2,1)S(1)} %copy-done.2), kind=kOutput, calls=%fused_computation.2 | convolution fusion | flops 3290169344 | bytes 8716288 | tf_op jit(solution)/shard_map/dot_general | solution.py:31
  346.0 13.1 %reduce-scatter.3.cloned.1.call-done = bf16[64,1792]{1,0:T(8,128)(2,1)} async-done(((bf16[1024,1792]{1,0:T(8,128)(2,1)}), bf16[64,1792]{1,0:T(8,128)(2,1)}) %reduce-scatter.3.cloned.1.call-update) | async-done | bytes 229392 | tf_op jit(solution)/shard_map/reduce_scatter | solution.py:96
  359.1 94.6 %reduce-scatter.5.cloned.1.call-done = bf16[64,1792]{1,0:T(8,128)(2,1)} async-done(((bf16[1024,1792]{1,0:T(8,128)(2,1)}), bf16[64,1792]{1,0:T(8,128)(2,1)}) %reduce-scatter.5.cloned.1.call-update) | async-done | bytes 229392 | tf_op jit(solution)/shard_map/reduce_scatter | solution.py:96
  454.9 1.5 collective-permute-start.6
  (64 shorter events, 21.2 us)
Async XLA Ops:
  7.2 29.7 %copy-start = (bf16[4096,256]{1,0:T(8,128)(2,1)S(1)}, bf16[4096,256]{1,0:T(8,128)(2,1)}, u32[]{:S(2)}) copy-start(bf16[4096,256]{1,0:T(8,128)(2,1)} %param.7) | copy-start | bytes 6291460
  7.2 71.2 %all-gather.3.cloned.1.call-start = ((), (), s32[]{:S(2)}) async-start(), calls=%async_computation.13 | async-start | bytes 1949696 | tf_op jit(solution)/shard_map/all_gather | solution.py:59
  8.5 4.3 collective-permute-start
  15.4 21.5 %all-to-all-start = ((bf16[16,128,256]{2,1,0:T(8,128)(2,1)}), bf16[16,128,256]{2,1,0:T(8,128)(2,1)S(1)}, u32[]{:S(2)}, u32[]{:S(2)}) async-start(bf16[16,128,256]{2,1,0:T(8,128)(2,1)} %broadcast_in_dim.16), calls=%async_computation | async-start | bytes 2097152 | tf_op jit(solution)/shard_map/all_to_all | solution.py:40
  19.8 113.4 %all-gather.5.cloned.1.call-start = ((), (), s32[]{:S(2)}) async-start(), calls=%async_computation.14 | async-start | bytes 1949696 | tf_op jit(solution)/shard_map/all_gather | solution.py:59
  19.9 40.5 %collective-permute-start.1 = (bf16[896,896]{1,0:T(8,128)(2,1)}, bf16[896,896]{1,0:T(8,128)(2,1)}, u32[]{:S(2)}, u32[]{:S(2)}) collective-permute-start(bf16[896,896]{1,0:T(8,128)(2,1)} %param.8), channel_id=1, source_target_pairs={{0,1},{1,0},{2,3},{3,2},{4,5},{5,4},{6,7},{7,6},{8,9},{9,8},{10,11... | collective-permute-start | bytes 4816904 | tf_op jit(solution)/shard_map/ppermute | solution.py:17
  56.2 21.1 %all-to-all-start.2 = ((bf16[4,4,2,2,32,256]{5,4,1,3,2,0:T(8,128)(2,1)}), bf16[4,4,2,2,32,256]{5,4,1,3,2,0:T(8,128)(2,1)S(1)}, u32[]{:S(2)}, u32[]{:S(2)}) async-start(bf16[4,4,2,2,32,256]{5,4,1,3,2,0:T(8,128)(2,1)} %broadcast_in_dim.19), calls=%async_computation.2 | async-start | bytes 2097152 | tf_op jit(solution)/shard_map/all_to_all | solution.py:40
  83.9 54.8 %all-to-all-start.3 = ((bf16[8,64,896]{2,1,0:T(8,128)(2,1)}), bf16[8,64,896]{2,1,0:T(8,128)(2,1)S(1)}, u32[]{:S(2)}, u32[]{:S(2)}) async-start(bf16[8,64,896]{2,1,0:T(8,128)(2,1)} %bitcast.63), calls=%async_computation.3 | async-start | bytes 1835008 | tf_op jit(solution)/shard_map/all_to_all | solution.py:44
  138.7 18.2 %all-to-all-start.5 = ((bf16[8,64,896]{2,1,0:T(8,128)(2,1)}), bf16[8,64,896]{2,1,0:T(8,128)(2,1)}, u32[]{:S(2)}, u32[]{:S(2)}) async-start(bf16[8,64,896]{2,1,0:T(8,128)(2,1)} %bitcast.62), calls=%async_computation.5 | async-start | bytes 1835008 | tf_op jit(solution)/shard_map/all_to_all | solution.py:44
  158.0 16.0 %all-to-all-start.4 = ((bf16[8,64,896]{2,1,0:T(8,128)(2,1)}), bf16[8,64,896]{2,1,0:T(8,128)(2,1)S(1)}, u32[]{:S(2)}, u32[]{:S(2)}) async-start(bf16[8,64,896]{2,1,0:T(8,128)(2,1)} %broadcast_in_dim.20), calls=%async_computation.4 | async-start | bytes 1835008 | tf_op jit(solution)/shard_map/all_to_all | solution.py:40
  175.0 15.6 %all-to-all-start.6 = ((bf16[8,64,896]{2,1,0:T(8,128)(2,1)}), bf16[8,64,896]{2,1,0:T(8,128)(2,1)}, u32[]{:S(2)}, u32[]{:S(2)}) async-start(bf16[8,64,896]{2,1,0:T(8,128)(2,1)} %broadcast_in_dim.21), calls=%async_computation.6 | async-start | bytes 1835008 | tf_op jit(solution)/shard_map/all_to_all | solution.py:40
  179.3 179.8 %reduce-scatter.3.cloned.1.call-start = ((), (), s32[]{:S(2)}) async-start(), calls=%async_computation.15 | async-start | bytes 3899392 | tf_op jit(solution)/shard_map/reduce_scatter | solution.py:96
  179.3 16.3 %collective-permute-start.2 = (bf16[512,896]{1,0:T(8,128)(2,1)S(1)}, bf16[512,896]{1,0:T(8,128)(2,1)}, u32[]{:S(2)}, u32[]{:S(2)}) collective-permute-start(bf16[512,896]{1,0:T(8,128)(2,1)S(1)} %bitcast.59), channel_id=1, source_target_pairs={{0,1},{1,0},{2,3},{3,2},{4,5},{5,4},{6,7},{7,6},{8,9},{9,8},{10,11... | collective-permute-start | bytes 2752520 | tf_op jit(solution)/shard_map/ppermute | solution.py:17
  190.6 6.3 %collective-permute-start.3 = (bf16[512,896]{1,0:T(8,128)(2,1)}, bf16[512,896]{1,0:T(8,128)(2,1)S(1)}, u32[]{:S(2)}, u32[]{:S(2)}) collective-permute-start(bf16[512,896]{1,0:T(8,128)(2,1)} %bitcast.13), channel_id=1, source_target_pairs={{0,1},{1,0},{2,3},{3,2},{4,5},{5,4},{6,7},{7,6},{8,9},{9,8},{10,11... | collective-permute-start | bytes 2752520 | tf_op jit(solution)/shard_map/ppermute | solution.py:17
  194.6 2.3 copy-start.3
  194.6 2.3 copy-start.4
  195.6 7.9 %collective-permute-start.4 = (bf16[16,128,256]{2,1,0:T(8,128)(2,1)S(1)}, bf16[16,128,256]{2,1,0:T(8,128)(2,1)S(1)}, u32[]{:S(2)}, u32[]{:S(2)}) collective-permute-start(bf16[16,128,256]{2,1,0:T(8,128)(2,1)S(1)} %get-tuple-element.7), channel_id=1, source_target_pairs={{0,1},{1,0},{2,3},{3,2},{4,5},{5,4},{6,7},{7,6},{8,9},{9,8},{10,11... | collective-permute-start | bytes 3145736 | tf_op jit(solution)/shard_map/ppermute | solution.py:17
  199.7 3.1 copy-start.9
  202.8 3.4 copy-start.5
  202.8 2.1 collective-permute-start.5
  204.9 1.3 copy-start.7
  232.8 25.7 %copy-start.1 = (bf16[1792,896]{1,0:T(8,128)(2,1)S(1)}, bf16[1792,896]{1,0:T(8,128)(2,1)}, u32[]{:S(2)}) copy-start(bf16[1792,896]{1,0:T(8,128)(2,1)} %pad_maximum_fusion.1) | copy-start | bytes 9633796
  263.8 1.0 copy-start.6
  263.8 1.2 copy-start.8
  263.9 189.9 %reduce-scatter.5.cloned.1.call-start = ((), (), s32[]{:S(2)}) async-start(), calls=%async_computation.16 | async-start | bytes 3899392 | tf_op jit(solution)/shard_map/reduce_scatter | solution.py:96
  304.0 36.6 %copy-start.2 = (bf16[1792,896]{1,0:T(8,128)(2,1)S(1)}, bf16[1792,896]{1,0:T(8,128)(2,1)}, u32[]{:S(2)}) copy-start(bf16[1792,896]{1,0:T(8,128)(2,1)} %pad_maximum_fusion.1) | copy-start | bytes 9633796
  454.9 2.7 collective-permute-start.6
Sparse Core Ops, SparseCore 0:
  13.6 58.2 all-gather.2
  74.9 58.2 all-gather.4
  264.0 95.0 reduce-scatter.2
  362.6 91.0 reduce-scatter.4

commit v2 on v1

--- a/solution.py
+++ b/solution.py
@@ -9,7 +9,7 @@
 damping = 0.1
 SIZES = {"x": 4, "zh": 4, "y": 4, "zl": 2, "c": 2}
 TOKEN_CHUNKS = 2
-WIDTHS = (64, 64)
+WIDTHS = (56, 40, 32)
 bf16 = jnp.bfloat16
 
 
@@ -40,10 +40,10 @@
     return lax.all_to_all(copies, axes, 0, 0, tiled=True)
 
 
-def reduce(value, axes):
+def reduce(value, axes, dtype=bf16):
     got = lax.all_to_all(value, axes, 0, 0, tiled=True)
     got = got.reshape((count(axes), -1) + value.shape[1:])
-    return jnp.sum(got.astype(jnp.float32), 0).astype(bf16)
+    return jnp.sum(got.astype(jnp.float32), 0).astype(dtype)
 
 
 def body(acts, grads, basis_in, basis_out, scale_old):
@@ -55,17 +55,20 @@
     out_chip = jnp.concatenate([basis_out, swap(basis_out)], 0)
 
     width = 64 // TOKEN_CHUNKS
+    line = gather(grads_chip, ("zh",))
     lines = [
-        lax.all_gather(grads_chip[m * width : (m + 1) * width], ("x", "zh"), axis=0, tiled=True)
+        lax.all_gather(line[:, m * width : (m + 1) * width].reshape(4 * width, 1792), "x", axis=0, tiled=True)
         for m in range(TOKEN_CHUNKS)
     ]
 
-    features = gather(acts, ("y", "zl", "c"))
+    features = gather(after(acts, line), ("y", "zl", "c"))
     act_local = dot(features, basis_in.reshape(16, 256, 256), ((0, 2), (0, 1))).astype(bf16)
     act_local = roll(act_local.reshape(2, 64, 256), c, 0).reshape(2, TOKEN_CHUNKS, width, 256)
-    act_proj = gather(gather(act_local, ("zh",)), ("x",))
+    act_line = gather(act_local, ("zh",))
+    out_chip = after(out_chip, act_line)
+    act_proj = lax.all_gather(act_line.reshape(512, 256), "x", axis=0)
+    act_proj = act_proj.reshape(4, 4, 2, TOKEN_CHUNKS, width, 256)
     act_proj = jnp.transpose(act_proj, (2, 3, 0, 1, 4, 5)).reshape(2048, 256)
-    out_chip = after(out_chip, act_proj)
 
     own, other = [], []
     for line in lines:
@@ -93,8 +96,9 @@
         piece = reduce(dot(rows, corrected_chip).astype(bf16), around)
         left = gather(piece, around).reshape(16 * width, 896)
         update = dot(left, out_chip, ((1,), (1,))).astype(bf16)
-        steps.append(lax.psum_scatter(update, ("x", "zh"), scatter_dimension=0, tiled=True))
-    step = (-math.sqrt(2048) * jnp.concatenate(steps, 0).astype(jnp.float32)).astype(bf16)
+        update = lax.psum_scatter(update, "x", scatter_dimension=0, tiled=True)
+        steps.append(reduce(update, ("zh",), jnp.float32))
+    step = (-math.sqrt(2048) * jnp.concatenate(steps, 0)).astype(bf16)
     both = jnp.stack([step[:, :896], swap(step[:, 896:])])
     return (scale_new, roll(both, c, 0).reshape(256, 896))
 

time: 466 us -> 416 us (0.89)
  blocking collectives: 143 us -> 83.6 us
  waiting for transfers between devices: 220 us -> 183 us
  starting transfers between devices: 38.6 us -> 70.7 us
  matrix products: 30.6 us -> 40.6 us
    reduce_scatter x2 -> x3, waiting for transfers between devices: 108 us -> 23.3 us  [body(): update = lax.psum_scatter(update, 'x', scatter_dimension=0, tiled=True)]
    all_to_all x2 -> x6, waiting for transfers between devices: 12.8 us -> 70.1 us  [reduce(): got = lax.all_to_all(value, axes, 0, 0, tiled=True)]
    all_to_all x2, blocking collectives: 63.7 us -> 31.8 us  [reduce(): got = lax.all_to_all(value, axes, 0, 0, tiled=True)]
    all_to_all x3 -> x2, blocking collectives: 79.3 us -> 51.8 us  [gather(): return lax.all_to_all(copies, axes, 0, 0, tiled=True)]
    all_to_all x2 -> x6, starting transfers between devices: 8.86 us -> 29.4 us  [reduce(): got = lax.all_to_all(value, axes, 0, 0, tiled=True)]
    all_gather x2 -> x3, waiting for transfers between devices: 45.8 us -> 30.5 us  [the longest x2 16.7 us: body(): lax.all_gather(line[:, m * width:(m + 1) * width].reshape(4 * width, 1792...]
    all_to_all x4 -> x6, starting transfers between devices: 16.6 us -> 27.4 us  [gather(): return lax.all_to_all(copies, axes, 0, 0, tiled=True)]
    dot_general x9 -> x11, matrix products: 30.6 us -> 40.6 us  [dot(): lax.dot_general(a, b, (dims, ((), ())), preferred_element_type=jnp.float32)]
  transfers between devices with their start and end apart: 17 -> 25, of which waited for: 12 -> 17; matrix products, arithmetic and copies ran while one was open for 8% -> 12% of each run, Pallas kernels for 0% -> 0%
where the time goes in v2:
time: 416 us; the launch traced here: 414 us
  waiting for transfers between devices  183 us (44%)
  blocking collectives  83.6 us (20%)
  starting transfers between devices  70.7 us (17%)
  matrix products  40.6 us (10%)
  between operations  14.4 us (3%)
  local copies, waits for them, and re-layouts  12 us (3%)
  other arithmetic  10.4 us (2%)
    all_to_all x6, waiting for transfers between devices, reduce(): got = lax.all_to_all(value, axes, 0, 0, tiled=True)  70.1 us
    all_to_all x6, waiting for transfers between devices, gather(): return lax.all_to_all(copies, axes, 0, 0, tiled=True)  54 us
    all_to_all x2, blocking collectives, gather(): return lax.all_to_all(copies, axes, 0, 0, tiled=True)  51.8 us
    dot_general x11, matrix products, dot(): lax.dot_general(a, b, (dims, ((), ())), preferred_element_type=jnp.float32)  40.6 us
    all_to_all x2, blocking collectives, reduce(): got = lax.all_to_all(value, axes, 0, 0, tiled=True)  31.8 us
    all_to_all x6, starting transfers between devices, reduce(): got = lax.all_to_all(value, axes, 0, 0, tiled=True)  29.4 us
    all_to_all x6, starting transfers between devices, gather(): return lax.all_to_all(copies, axes, 0, 0, tiled=True)  27.4 us
    reduce_scatter x3, waiting for transfers between devices, body(): update = lax.psum_scatter(update, 'x', scatter_dimension=0, tiled=True)  23.3 us
  transfers between devices with their start and end apart: 25, of which 17 were waited for; matrix products, arithmetic and copies ran while one was open for 12% of the time, Pallas kernels for 0%

profile of v2, /device:TPU:1, one launch (start us, length us, event | category | flops | bytes accessed | tf_op | source)
XLA Modules:
  0.0 414.4 jit_solution(9885715787918602190)
XLA Ops:
  12.7 29.2 %all_to_all.112 = bf16[4,64,1792]{2,1,0:T(8,128)(2,1)S(1)} all-to-all(bf16[4,64,1792]{2,1,0:T(8,128)(2,1)S(1)} %broadcast_in_dim.18), channel_id=1, replica_groups=mesh['x'=4,'zh'=4,'y'=4,'zl'=2,'c'=2] {'zh'}, dimensions={0} | all-to-all | bytes 1835008 | tf_op jit(solution)/shard_map/all_to_all | solution.py:40
  44.0 7.8 %all-to-all-start.1 = ((bf16[16,128,256]{2,1,0:T(8,128)(2,1)}), bf16[16,128,256]{2,1,0:T(8,128)(2,1)S(1)}, u32[]{:S(2)}, u32[]{:S(2)}) async-start(bf16[16,128,256]{2,1,0:T(8,128)(2,1)} %broadcast_in_dim.19), calls=%async_computation.1 | async-start | bytes 2097152 | tf_op jit(solution)/shard_map/all_to_all | solution.py:40
  52.5 15.1 %all-to-all-done.1 = bf16[16,128,256]{2,1,0:T(8,128)(2,1)S(1)} async-done(((bf16[16,128,256]{2,1,0:T(8,128)(2,1)}), bf16[16,128,256]{2,1,0:T(8,128)(2,1)S(1)}, u32[]{:S(2)}, u32[]{:S(2)}) %all-to-all-start.1) | async-done | bytes 1048608 | tf_op jit(solution)/shard_map/all_to_all | solution.py:40
  76.1 4.5 %all-to-all-done.2 = bf16[4,2,2,32,256]{4,3,2,1,0:T(8,128)(2,1)S(1)} async-done(((bf16[4,2,2,32,256]{4,3,2,1,0:T(8,128)(2,1)}), bf16[4,2,2,32,256]{4,3,2,1,0:T(8,128)(2,1)S(1)}, u32[]{:S(2)}, u32[]{:S(2)}) %all-to-all-start.2) | async-done | bytes 262176 | tf_op jit(solution)/shard_map/all_to_all | solution.py:40
  80.6 5.5 %convolution_convert_fusion.5 = bf16[512,896]{1,0:T(8,128)(2,1)} fusion(bf16[512,1792]{1,0:T(8,128)(2,1)} %all-gather.8.cloned.1.call-done, bf16[1792,896]{1,0:T(8,128)(2,1)} %pad_maximum_fusion.1), kind=kOutput, calls=%fused_computation.17 | convolution fusion | flops 1644625920 | bytes 5963776 | tf_op jit(solution)/shard_map/dot_general | solution.py:31
  86.2 4.8 %all-to-all-start.5 = ((bf16[8,64,896]{2,1,0:T(8,128)(2,1)}), bf16[8,64,896]{2,1,0:T(8,128)(2,1)S(1)}, u32[]{:S(2)}, u32[]{:S(2)}) async-start(bf16[8,64,896]{2,1,0:T(8,128)(2,1)} %bitcast.74), calls=%async_computation.5 | async-start | bytes 1835008 | tf_op jit(solution)/shard_map/all_to_all | solution.py:44
  90.9 16.7 %all-gather.6.cloned.1.call-done = bf16[512,1792]{1,0:T(8,128)(2,1)} async-done(((bf16[128,1792]{1,0:T(8,128)(2,1)}), bf16[512,1792]{1,0:T(8,128)(2,1)}) %all-gather.6.cloned.1.call-update) | async-done | bytes 1835024 | tf_op jit(solution)/shard_map/all_gather | solution.py:60
  107.6 5.5 %convolution_convert_fusion.6 = bf16[512,896]{1,0:T(8,128)(2,1)} fusion(bf16[512,1792]{1,0:T(8,128)(2,1)} %all-gather.6.cloned.1.call-done, bf16[1792,896]{1,0:T(8,128)(2,1)} %pad_maximum_fusion.1), kind=kOutput, calls=%fused_computation.18 | convolution fusion | flops 1644625920 | bytes 5963776 | tf_op jit(solution)/shard_map/dot_general | solution.py:31
  113.1 5.0 %all-to-all-start.3 = ((bf16[8,64,896]{2,1,0:T(8,128)(2,1)}), bf16[8,64,896]{2,1,0:T(8,128)(2,1)}, u32[]{:S(2)}, u32[]{:S(2)}) async-start(bf16[8,64,896]{2,1,0:T(8,128)(2,1)} %bitcast.73), calls=%async_computation.3 | async-start | bytes 1835008 | tf_op jit(solution)/shard_map/all_to_all | solution.py:44
  118.2 13.1 %all-to-all-done.3 = bf16[8,64,896]{2,1,0:T(8,128)(2,1)} async-done(((bf16[8,64,896]{2,1,0:T(8,128)(2,1)}), bf16[8,64,896]{2,1,0:T(8,128)(2,1)}, u32[]{:S(2)}, u32[]{:S(2)}) %all-to-all-start.3) | async-done | bytes 917536 | tf_op jit(solution)/shard_map/all_to_all | solution.py:44
  132.3 4.2 %all-to-all-start.6 = ((bf16[8,64,896]{2,1,0:T(8,128)(2,1)}), bf16[8,64,896]{2,1,0:T(8,128)(2,1)}, u32[]{:S(2)}, u32[]{:S(2)}) async-start(bf16[8,64,896]{2,1,0:T(8,128)(2,1)} %broadcast_in_dim.23), calls=%async_computation.6 | async-start | bytes 1835008 | tf_op jit(solution)/shard_map/all_to_all | solution.py:40
  137.9 11.0 %all-to-all-done.6 = bf16[8,64,896]{2,1,0:T(8,128)(2,1)} async-done(((bf16[8,64,896]{2,1,0:T(8,128)(2,1)}), bf16[8,64,896]{2,1,0:T(8,128)(2,1)}, u32[]{:S(2)}, u32[]{:S(2)}) %all-to-all-start.6) | async-done | bytes 917536 | tf_op jit(solution)/shard_map/all_to_all | solution.py:40
  149.9 4.2 %all-to-all-start.4 = ((bf16[8,64,896]{2,1,0:T(8,128)(2,1)}), bf16[8,64,896]{2,1,0:T(8,128)(2,1)}, u32[]{:S(2)}, u32[]{:S(2)}) async-start(bf16[8,64,896]{2,1,0:T(8,128)(2,1)} %broadcast_in_dim.22), calls=%async_computation.4 | async-start | bytes 1835008 | tf_op jit(solution)/shard_map/all_to_all | solution.py:40
  158.0 7.5 %all-to-all-done.4 = bf16[8,64,896]{2,1,0:T(8,128)(2,1)} async-done(((bf16[8,64,896]{2,1,0:T(8,128)(2,1)}), bf16[8,64,896]{2,1,0:T(8,128)(2,1)}, u32[]{:S(2)}, u32[]{:S(2)}) %all-to-all-start.4) | async-done | bytes 917536 | tf_op jit(solution)/shard_map/all_to_all | solution.py:40
  170.6 13.8 %all-gather.4.cloned.1.call-done = bf16[4,512,256]{2,1,0:T(8,128)(2,1)} async-done(((bf16[1,512,256]{2,1,0:T(8,128)(2,1)}), bf16[4,512,256]{2,1,0:T(8,128)(2,1)}) %all-gather.4.cloned.1.call-update) | async-done | bytes 1048592 | tf_op jit(solution)/shard_map/all_gather | solution.py:69
  197.8 5.1 %all-to-all-start.13 = ((bf16[8,64,896]{2,1,0:T(8,128)(2,1)}), bf16[8,64,896]{2,1,0:T(8,128)(2,1)S(1)}, u32[]{:S(2)}, u32[]{:S(2)}) async-start(bf16[8,64,896]{2,1,0:T(8,128)(2,1)} %bitcast.75), calls=%async_computation.15 | async-start | bytes 1835008 | tf_op jit(solution)/shard_map/all_to_all | solution.py:44
  205.9 10.9 %all-to-all-done.13 = bf16[8,64,896]{2,1,0:T(8,128)(2,1)S(1)} async-done(((bf16[8,64,896]{2,1,0:T(8,128)(2,1)}), bf16[8,64,896]{2,1,0:T(8,128)(2,1)S(1)}, u32[]{:S(2)}, u32[]{:S(2)}) %all-to-all-start.13) | async-done | bytes 917536 | tf_op jit(solution)/shard_map/all_to_all | solution.py:44
  222.6 13.6 %all-to-all-done.10 = bf16[8,80,896]{2,1,0:T(8,128)(2,1)S(1)} async-done(((bf16[8,80,896]{2,1,0:T(8,128)(2,1)}), bf16[8,80,896]{2,1,0:T(8,128)(2,1)S(1)}, u32[]{:S(2)}, u32[]{:S(2)}) %all-to-all-start.10) | async-done | bytes 1146912 | tf_op jit(solution)/shard_map/all_to_all | solution.py:44
  237.2 4.2 %all-to-all-start.14 = ((bf16[8,64,896]{2,1,0:T(8,128)(2,1)}), bf16[8,64,896]{2,1,0:T(8,128)(2,1)}, u32[]{:S(2)}, u32[]{:S(2)}) async-start(bf16[8,64,896]{2,1,0:T(8,128)(2,1)} %broadcast_in_dim.26), calls=%async_computation.16 | async-start | bytes 1835008 | tf_op jit(solution)/shard_map/all_to_all | solution.py:40
  241.7 11.7 %all-to-all-done.14 = bf16[8,64,896]{2,1,0:T(8,128)(2,1)} async-done(((bf16[8,64,896]{2,1,0:T(8,128)(2,1)}), bf16[8,64,896]{2,1,0:T(8,128)(2,1)}, u32[]{:S(2)}, u32[]{:S(2)}) %all-to-all-start.14) | async-done | bytes 917536 | tf_op jit(solution)/shard_map/all_to_all | solution.py:40
  258.1 5.5 %convolution_convert_fusion.2 = bf16[512,1792]{1,0:T(8,128)(2,1)} fusion(bf16[512,896]{1,0:T(8,128)(2,1)} %bitcast.30, bf16[1792,896]{1,0:T(8,128)(2,1)} %pad_maximum_fusion.1), kind=kOutput, calls=%fused_computation.8 | convolution fusion | flops 1645084672 | bytes 5963776 | tf_op jit(solution)/shard_map/dot_general | solution.py:31
  267.2 4.2 %all-to-all-done.11 = bf16[8,80,896]{2,1,0:T(8,128)(2,1)S(1)} async-done(((bf16[8,80,896]{2,1,0:T(8,128)(2,1)}), bf16[8,80,896]{2,1,0:T(8,128)(2,1)S(1)}, u32[]{:S(2)}, u32[]{:S(2)}) %all-to-all-start.11) | async-done | bytes 1146912 | tf_op jit(solution)/shard_map/all_to_all | solution.py:40
  271.4 4.2 %all-to-all-start.7 = ((bf16[8,112,896]{2,1,0:T(8,128)(2,1)}), bf16[8,112,896]{2,1,0:T(8,128)(2,1)S(1)}, u32[]{:S(2)}, u32[]{:S(2)}) async-start(bf16[8,112,896]{2,1,0:T(8,128)(2,1)} %bitcast.21), calls=%async_computation.7 | async-start | bytes 3211264 | tf_op jit(solution)/shard_map/all_to_all | solution.py:44
  275.6 5.9 %convolution_convert_fusion.1 = bf16[640,1792]{1,0:T(8,128)(2,1)} fusion(bf16[640,896]{1,0:T(8,128)(2,1)S(1)} %bitcast.67, bf16[1792,896]{1,0:T(8,128)(2,1)} %pad_maximum_fusion.1), kind=kOutput, calls=%fused_computation.7 | convolution fusion | flops 2056355840 | bytes 6651904 | tf_op jit(solution)/shard_map/dot_general | solution.py:31
  281.5 12.0 %all-to-all-done.7 = bf16[8,112,896]{2,1,0:T(8,128)(2,1)S(1)} async-done(((bf16[8,112,896]{2,1,0:T(8,128)(2,1)}), bf16[8,112,896]{2,1,0:T(8,128)(2,1)S(1)}, u32[]{:S(2)}, u32[]{:S(2)}) %all-to-all-start.7) | async-done | bytes 1605664 | tf_op jit(solution)/shard_map/all_to_all | solution.py:44
  293.9 22.6 %all_to_all.113 = bf16[8,112,896]{2,1,0:T(8,128)(2,1)S(1)} all-to-all(bf16[8,112,896]{2,1,0:T(8,128)(2,1)S(1)} %broadcast_in_dim.24), channel_id=1, replica_groups=mesh['x'=4,'zh'=4,'y'=4,'zl'=2,'c'=2] {'y','zl'}, dimensions={0} | all-to-all | bytes 3211264 | tf_op jit(solution)/shard_map/all_to_all | solution.py:40
  316.5 4.9 %convolution_convert_fusion = bf16[896,1792]{1,0:T(8,128)(2,1)} fusion(bf16[896,896]{1,0:T(8,128)(2,1)S(1)} %bitcast.66, bf16[1792,896]{1,0:T(8,128)(2,1)S(1)} %copy-done.2), kind=kOutput, calls=%fused_computation.5 | convolution fusion | flops 2878898176 | bytes 8028160 | tf_op jit(solution)/shard_map/dot_general | solution.py:31
  321.4 16.2 %all_to_all.114 = bf16[4,32,1792]{2,1,0:T(8,128)(2,1)S(1)} all-to-all(bf16[4,32,1792]{2,1,0:T(8,128)(2,1)} %bitcast.81), channel_id=1, replica_groups=mesh['x'=4,'zh'=4,'y'=4,'zl'=2,'c'=2] {'zh'}, dimensions={0} | all-to-all | bytes 917504 | tf_op jit(solution)/shard_map/all_to_all | solution.py:44
  337.6 15.6 %all_to_all.115 = bf16[4,40,1792]{2,1,0:T(8,128)(2,1)S(1)} all-to-all(bf16[4,40,1792]{2,1,0:T(8,128)(2,1)} %bitcast.79), channel_id=1, replica_groups=mesh['x'=4,'zh'=4,'y'=4,'zl'=2,'c'=2] {'zh'}, dimensions={0} | all-to-all | bytes 1146880 | tf_op jit(solution)/shard_map/all_to_all | solution.py:44
  353.2 23.2 %reduce-scatter.4.cloned.1.call-done = bf16[224,1792]{1,0:T(8,128)(2,1)} async-done(((bf16[896,1792]{1,0:T(8,128)(2,1)}), bf16[224,1792]{1,0:T(8,128)(2,1)}) %reduce-scatter.4.cloned.1.call-update) | async-done | bytes 802832 | tf_op jit(solution)/shard_map/reduce_scatter | solution.py:99
  376.4 6.7 %all-to-all-start.9 = ((bf16[4,56,1792]{2,1,0:T(8,128)(2,1)}), bf16[4,56,1792]{2,1,0:T(8,128)(2,1)S(1)}, u32[]{:S(2)}, u32[]{:S(2)}) async-start(bf16[4,56,1792]{2,1,0:T(8,128)(2,1)} %bitcast.77), calls=%async_computation.10 | async-start | bytes 1605632 | tf_op jit(solution)/shard_map/all_to_all | solution.py:44
  383.3 20.6 %all-to-all-done.9 = bf16[4,56,1792]{2,1,0:T(8,128)(2,1)S(1)} async-done(((bf16[4,56,1792]{2,1,0:T(8,128)(2,1)}), bf16[4,56,1792]{2,1,0:T(8,128)(2,1)S(1)}, u32[]{:S(2)}, u32[]{:S(2)}) %all-to-all-start.9) | async-done | bytes 802848 | tf_op jit(solution)/shard_map/all_to_all | solution.py:44
  (96 shorter events, 64.9 us)
Async XLA Ops:
  7.2 73.5 %all-gather.8.cloned.1.call-start = ((), (), s32[]{:S(2)}) async-start(), calls=%async_computation.21 | async-start | bytes 2293760 | tf_op jit(solution)/shard_map/all_gather | solution.py:60
  8.3 4.3 %collective-permute-start = (bf16[64,896]{1,0:T(8,128)(2,1)S(1)}, bf16[64,896]{1,0:T(8,128)(2,1)S(1)}, u32[]{:S(2)}, u32[]{:S(2)}) collective-permute-start(bf16[64,896]{1,0:T(8,128)(2,1)S(1)} %get-tuple-element.13), channel_id=1, source_target_pairs={{0,1},{1,0},{2,3},{3,2},{4,5},{5,4},{6,7},{7,6},{8,9},{9,8},{10,11... | collective-permute-start | bytes 344072 | tf_op jit(solution)/shard_map/ppermute | solution.py:17
  12.7 30.3 %copy-start.4 = (bf16[128,256]{1,0:T(8,128)(2,1)S(1)}, bf16[128,256]{1,0:T(8,128)(2,1)}, u32[]{:S(2)}) copy-start(bf16[128,256]{1,0:T(8,128)(2,1)} %param.5) | copy-start | bytes 196612
  42.9 24.7 %copy-start = (bf16[4096,256]{1,0:T(8,128)(2,1)S(1)}, bf16[4096,256]{1,0:T(8,128)(2,1)}, u32[]{:S(2)}) copy-start(bf16[4096,256]{1,0:T(8,128)(2,1)} %param.7) | copy-start | bytes 6291460
  44.0 23.6 %all-to-all-start.1 = ((bf16[16,128,256]{2,1,0:T(8,128)(2,1)}), bf16[16,128,256]{2,1,0:T(8,128)(2,1)S(1)}, u32[]{:S(2)}, u32[]{:S(2)}) async-start(bf16[16,128,256]{2,1,0:T(8,128)(2,1)} %broadcast_in_dim.19), calls=%async_computation.1 | async-start | bytes 2097152 | tf_op jit(solution)/shard_map/all_to_all | solution.py:40
  51.8 55.9 %all-gather.6.cloned.1.call-start = ((), (), s32[]{:S(2)}) async-start(), calls=%async_computation.20 | async-start | bytes 2293760 | tf_op jit(solution)/shard_map/all_gather | solution.py:60
  51.8 20.4 %collective-permute-start.1 = (bf16[896,896]{1,0:T(8,128)(2,1)}, bf16[896,896]{1,0:T(8,128)(2,1)}, u32[]{:S(2)}, u32[]{:S(2)}) collective-permute-start(bf16[896,896]{1,0:T(8,128)(2,1)} %param.8), channel_id=1, source_target_pairs={{0,1},{1,0},{2,3},{3,2},{4,5},{5,4},{6,7},{7,6},{8,9},{9,8},{10,11... | collective-permute-start | bytes 4816904 | tf_op jit(solution)/shard_map/ppermute | solution.py:17
  68.9 11.8 %all-to-all-start.2 = ((bf16[4,2,2,32,256]{4,3,2,1,0:T(8,128)(2,1)}), bf16[4,2,2,32,256]{4,3,2,1,0:T(8,128)(2,1)S(1)}, u32[]{:S(2)}, u32[]{:S(2)}) async-start(bf16[4,2,2,32,256]{4,3,2,1,0:T(8,128)(2,1)} %broadcast_in_dim.21), calls=%async_computation.2 | async-start | bytes 524288 | tf_op jit(solution)/shard_map/all_to_all | solution.py:40
  80.6 5.5 %copy-start.3 = (bf16[4,2,2,32,256]{4,3,2,1,0:T(8,128)(2,1)}, bf16[4,2,2,32,256]{4,3,2,1,0:T(8,128)(2,1)S(1)}, u32[]{:S(2)}) copy-start(bf16[4,2,2,32,256]{4,3,2,1,0:T(8,128)(2,1)S(1)} %all-to-all-done.2) | copy-start | bytes 786436
  86.2 26.9 %all-to-all-start.5 = ((bf16[8,64,896]{2,1,0:T(8,128)(2,1)}), bf16[8,64,896]{2,1,0:T(8,128)(2,1)S(1)}, u32[]{:S(2)}, u32[]{:S(2)}) async-start(bf16[8,64,896]{2,1,0:T(8,128)(2,1)} %bitcast.74), calls=%async_computation.5 | async-start | bytes 1835008 | tf_op jit(solution)/shard_map/all_to_all | solution.py:44
  113.1 18.2 %all-to-all-start.3 = ((bf16[8,64,896]{2,1,0:T(8,128)(2,1)}), bf16[8,64,896]{2,1,0:T(8,128)(2,1)}, u32[]{:S(2)}, u32[]{:S(2)}) async-start(bf16[8,64,896]{2,1,0:T(8,128)(2,1)} %bitcast.73), calls=%async_computation.3 | async-start | bytes 1835008 | tf_op jit(solution)/shard_map/all_to_all | solution.py:44
  132.3 16.5 %all-to-all-start.6 = ((bf16[8,64,896]{2,1,0:T(8,128)(2,1)}), bf16[8,64,896]{2,1,0:T(8,128)(2,1)}, u32[]{:S(2)}, u32[]{:S(2)}) async-start(bf16[8,64,896]{2,1,0:T(8,128)(2,1)} %broadcast_in_dim.23), calls=%async_computation.6 | async-start | bytes 1835008 | tf_op jit(solution)/shard_map/all_to_all | solution.py:40
  149.9 15.6 %all-to-all-start.4 = ((bf16[8,64,896]{2,1,0:T(8,128)(2,1)}), bf16[8,64,896]{2,1,0:T(8,128)(2,1)}, u32[]{:S(2)}, u32[]{:S(2)}) async-start(bf16[8,64,896]{2,1,0:T(8,128)(2,1)} %broadcast_in_dim.22), calls=%async_computation.4 | async-start | bytes 1835008 | tf_op jit(solution)/shard_map/all_to_all | solution.py:40
  154.1 30.2 %all-gather.4.cloned.1.call-start = ((), (), s32[]{:S(2)}) async-start(), calls=%async_computation.19 | async-start | bytes 1310720 | tf_op jit(solution)/shard_map/all_gather | solution.py:69
  154.9 30.9 %collective-permute-start.3 = (bf16[512,896]{1,0:T(8,128)(2,1)}, bf16[512,896]{1,0:T(8,128)(2,1)}, u32[]{:S(2)}, u32[]{:S(2)}) collective-permute-start(bf16[512,896]{1,0:T(8,128)(2,1)} %bitcast.16), channel_id=1, source_target_pairs={{0,1},{1,0},{2,3},{3,2},{4,5},{5,4},{6,7},{7,6},{8,9},{9,8},{10,11... | collective-permute-start | bytes 2752520 | tf_op jit(solution)/shard_map/ppermute | solution.py:17
  165.5 20.3 %collective-permute-start.2 = (bf16[512,896]{1,0:T(8,128)(2,1)}, bf16[512,896]{1,0:T(8,128)(2,1)}, u32[]{:S(2)}, u32[]{:S(2)}) collective-permute-start(bf16[512,896]{1,0:T(8,128)(2,1)} %bitcast.13), channel_id=1, source_target_pairs={{0,1},{1,0},{2,3},{3,2},{4,5},{5,4},{6,7},{7,6},{8,9},{9,8},{10,11... | collective-permute-start | bytes 2752520 | tf_op jit(solution)/shard_map/ppermute | solution.py:17
  170.5 24.3 %collective-permute-start.4 = (bf16[16,128,256]{2,1,0:T(8,128)(2,1)S(1)}, bf16[16,128,256]{2,1,0:T(8,128)(2,1)S(1)}, u32[]{:S(2)}, u32[]{:S(2)}) collective-permute-start(bf16[16,128,256]{2,1,0:T(8,128)(2,1)S(1)} %get-tuple-element.7), channel_id=1, source_target_pairs={{0,1},{1,0},{2,3},{3,2},{4,5},{5,4},{6,7},{7,6},{8,9},{9,8},{10,11... | collective-permute-start | bytes 3145736 | tf_op jit(solution)/shard_map/ppermute | solution.py:17
  189.2 3.6 copy-start.12
  192.8 5.0 %copy-start.6 = (bf16[256,896]{1,0:T(8,128)(2,1)}, bf16[256,896]{1,0:T(8,128)(2,1)S(1)}, u32[]{:S(2)}) copy-start(bf16[256,896]{1,0:T(8,128)(2,1)S(1)} %fusion.10) | copy-start | bytes 1376260
  192.9 3.3 collective-permute-start.5
  197.8 5.2 %copy-start.7 = (bf16[256,896]{1,0:T(8,128)(2,1)S(1)}, bf16[256,896]{1,0:T(8,128)(2,1)}, u32[]{:S(2)}) copy-start(bf16[256,896]{1,0:T(8,128)(2,1)} %copy-done.6) | copy-start | bytes 1376260
  197.8 18.9 %all-to-all-start.13 = ((bf16[8,64,896]{2,1,0:T(8,128)(2,1)}), bf16[8,64,896]{2,1,0:T(8,128)(2,1)S(1)}, u32[]{:S(2)}, u32[]{:S(2)}) async-start(bf16[8,64,896]{2,1,0:T(8,128)(2,1)} %bitcast.75), calls=%async_computation.15 | async-start | bytes 1835008 | tf_op jit(solution)/shard_map/all_to_all | solution.py:44
  217.7 18.5 %all-to-all-start.10 = ((bf16[8,80,896]{2,1,0:T(8,128)(2,1)}), bf16[8,80,896]{2,1,0:T(8,128)(2,1)S(1)}, u32[]{:S(2)}, u32[]{:S(2)}) async-start(bf16[8,80,896]{2,1,0:T(8,128)(2,1)} %bitcast.68), calls=%async_computation.11 | async-start | bytes 2293760 | tf_op jit(solution)/shard_map/all_to_all | solution.py:44
  237.2 16.1 %all-to-all-start.14 = ((bf16[8,64,896]{2,1,0:T(8,128)(2,1)}), bf16[8,64,896]{2,1,0:T(8,128)(2,1)}, u32[]{:S(2)}, u32[]{:S(2)}) async-start(bf16[8,64,896]{2,1,0:T(8,128)(2,1)} %broadcast_in_dim.26), calls=%async_computation.16 | async-start | bytes 1835008 | tf_op jit(solution)/shard_map/all_to_all | solution.py:40
  254.5 16.9 %all-to-all-start.11 = ((bf16[8,80,896]{2,1,0:T(8,128)(2,1)}), bf16[8,80,896]{2,1,0:T(8,128)(2,1)S(1)}, u32[]{:S(2)}, u32[]{:S(2)}) async-start(bf16[8,80,896]{2,1,0:T(8,128)(2,1)} %broadcast_in_dim.25), calls=%async_computation.12 | async-start | bytes 2293760 | tf_op jit(solution)/shard_map/all_to_all | solution.py:40
  258.1 63.3 %reduce-scatter.8.cloned.1.call-start = ((), (), s32[]{:S(2)}) async-start(), calls=%async_computation.24 | async-start | bytes 2293760 | tf_op jit(solution)/shard_map/reduce_scatter | solution.py:99
  271.4 22.1 %all-to-all-start.7 = ((bf16[8,112,896]{2,1,0:T(8,128)(2,1)}), bf16[8,112,896]{2,1,0:T(8,128)(2,1)S(1)}, u32[]{:S(2)}, u32[]{:S(2)}) async-start(bf16[8,112,896]{2,1,0:T(8,128)(2,1)} %bitcast.21), calls=%async_computation.7 | async-start | bytes 3211264 | tf_op jit(solution)/shard_map/all_to_all | solution.py:44
  275.5 62.0 %reduce-scatter.6.cloned.1.call-start = ((), (), s32[]{:S(2)}) async-start(), calls=%async_computation.23 | async-start | bytes 2867200 | tf_op jit(solution)/shard_map/reduce_scatter | solution.py:99
  281.5 94.9 %reduce-scatter.4.cloned.1.call-start = ((), (), s32[]{:S(2)}) async-start(), calls=%async_computation.22 | async-start | bytes 4014080 | tf_op jit(solution)/shard_map/reduce_scatter | solution.py:99
  293.8 22.7 %copy-start.2 = (bf16[1792,896]{1,0:T(8,128)(2,1)S(1)}, bf16[1792,896]{1,0:T(8,128)(2,1)}, u32[]{:S(2)}) copy-start(bf16[1792,896]{1,0:T(8,128)(2,1)} %pad_maximum_fusion.1) | copy-start | bytes 9633796
  376.4 27.5 %all-to-all-start.9 = ((bf16[4,56,1792]{2,1,0:T(8,128)(2,1)}), bf16[4,56,1792]{2,1,0:T(8,128)(2,1)S(1)}, u32[]{:S(2)}, u32[]{:S(2)}) async-start(bf16[4,56,1792]{2,1,0:T(8,128)(2,1)} %bitcast.77), calls=%async_computation.10 | async-start | bytes 1605632 | tf_op jit(solution)/shard_map/all_to_all | solution.py:44
  404.2 2.3 collective-permute-start.6
  (6 other events, 7.4 us)
Sparse Core Ops, SparseCore 0:
  43.1 30.9 all-gather.7
  76.4 31.1 all-gather.5
  156.8 27.5 all-gather.3
  263.8 32.8 reduce-scatter.7
  299.1 33.5 reduce-scatter.5
  335.3 41.0 reduce-scatter.3

commit v3 on v2

--- a/solution.py
+++ b/solution.py
@@ -8,8 +8,7 @@
 decay_rate = 0.5
 damping = 0.1
 SIZES = {"x": 4, "zh": 4, "y": 4, "zl": 2, "c": 2}
-TOKEN_CHUNKS = 2
-WIDTHS = (56, 40, 32)
+WIDTHS = (80, 48)
 bf16 = jnp.bfloat16
 
 
@@ -54,28 +53,18 @@
     grads_chip = jnp.concatenate([halves[0], swap(halves[1])], 1)
     out_chip = jnp.concatenate([basis_out, swap(basis_out)], 0)
 
-    width = 64 // TOKEN_CHUNKS
-    line = gather(grads_chip, ("zh",))
-    lines = [
-        lax.all_gather(line[:, m * width : (m + 1) * width].reshape(4 * width, 1792), "x", axis=0, tiled=True)
-        for m in range(TOKEN_CHUNKS)
-    ]
+    features = lax.all_gather(acts, ("y", "zl", "c"), axis=1, tiled=True)
+    act_local = roll(dot(features, basis_in).astype(bf16).reshape(2, 64, 256), c, 0)
+    act_line = gather(act_local, ("zh",))
 
-    features = gather(after(acts, line), ("y", "zl", "c"))
-    act_local = dot(features, basis_in.reshape(16, 256, 256), ((0, 2), (0, 1))).astype(bf16)
-    act_local = roll(act_local.reshape(2, 64, 256), c, 0).reshape(2, TOKEN_CHUNKS, width, 256)
-    act_line = gather(act_local, ("zh",))
-    out_chip = after(out_chip, act_line)
-    act_proj = lax.all_gather(act_line.reshape(512, 256), "x", axis=0)
-    act_proj = act_proj.reshape(4, 4, 2, TOKEN_CHUNKS, width, 256)
-    act_proj = jnp.transpose(act_proj, (2, 3, 0, 1, 4, 5)).reshape(2048, 256)
+    line = after(gather(grads_chip, ("zh",)), act_local).reshape(256, 1792)
+    line = lax.all_gather(line, "x", axis=0, tiled=True)
+    act_proj = lax.all_gather(act_line.reshape(512, 256), "x", axis=0).reshape(4, 4, 2, 64, 256)
+    act_proj = jnp.transpose(act_proj, (2, 0, 1, 3, 4)).reshape(2048, 256)
 
-    own, other = [], []
-    for line in lines:
-        term = dot(line, out_chip).astype(bf16)
-        own.append(gather(reduce(term, around), around).reshape(-1, 896))
-        other.append(swap(own[-1]))
-    grad_proj = jnp.concatenate(own + other, 0)
+    piece = reduce(dot(line, after(out_chip, act_line)).astype(bf16), around)
+    grad_half = gather(after(piece, act_proj), around).reshape(1024, 896)
+    grad_proj = jnp.concatenate([grad_half, swap(grad_half)], 0)
 
     act_square = act_proj * act_proj
     grad_square = grad_proj * grad_proj
@@ -96,6 +85,7 @@
         piece = reduce(dot(rows, corrected_chip).astype(bf16), around)
         left = gather(piece, around).reshape(16 * width, 896)
         update = dot(left, out_chip, ((1,), (1,))).astype(bf16)
+        corrected_chip = after(corrected_chip, update)
         update = lax.psum_scatter(update, "x", scatter_dimension=0, tiled=True)
         steps.append(reduce(update, ("zh",), jnp.float32))
     step = (-math.sqrt(2048) * jnp.concatenate(steps, 0)).astype(bf16)

time: 416 us -> 389 us (0.935)
  blocking collectives: 83.6 us -> 126 us
  starting transfers between devices: 70.7 us -> 40.9 us
  waiting for transfers between devices: 183 us -> 158 us
  matrix products: 40.6 us -> 29.8 us
    all_gather x3, waiting for transfers between devices: 30.5 us -> 91.5 us  [the longest x1 34.8 us: body(): features = lax.all_gather(acts, ('y', 'zl', 'c'), axis=1, tiled=True)]
    all_to_all x6 -> x3, waiting for transfers between devices: 70.1 us -> 17.6 us  [reduce(): got = lax.all_to_all(value, axes, 0, 0, tiled=True)]
    all_to_all x6 -> x2, waiting for transfers between devices: 54 us -> 3.55 us  [gather(): return lax.all_to_all(copies, axes, 0, 0, tiled=True)]
    all_to_all x2 -> x3, blocking collectives: 51.8 us -> 76 us  [gather(): return lax.all_to_all(copies, axes, 0, 0, tiled=True)]
    all_to_all x2, blocking collectives: 31.8 us -> 50.3 us  [reduce(): got = lax.all_to_all(value, axes, 0, 0, tiled=True)]
    reduce_scatter x3 -> x2, waiting for transfers between devices: 23.3 us -> 38.2 us  [body(): update = lax.psum_scatter(update, 'x', scatter_dimension=0, tiled=True)]
    all_to_all x6 -> x2, starting transfers between devices: 27.4 us -> 13.3 us  [gather(): return lax.all_to_all(copies, axes, 0, 0, tiled=True)]
    all_to_all x6 -> x3, starting transfers between devices: 29.4 us -> 18.4 us  [reduce(): got = lax.all_to_all(value, axes, 0, 0, tiled=True)]
  transfers between devices with their start and end apart: 25 -> 16, of which waited for: 17 -> 11; matrix products, arithmetic and copies ran while one was open for 12% -> 6% of each run, Pallas kernels for 0% -> 0%
where the time goes in v3:
time: 389 us; the launch traced here: 388 us
  waiting for transfers between devices  158 us (41%)
  blocking collectives  126 us (32%)
  starting transfers between devices  40.9 us (11%)
  matrix products  29.8 us (8%)
  between operations  14 us (4%)
  local copies, waits for them, and re-layouts  12.6 us (3%)
  other arithmetic  6.77 us (2%)
    all_to_all x3, blocking collectives, gather(): return lax.all_to_all(copies, axes, 0, 0, tiled=True)  76 us
    all_to_all x2, blocking collectives, reduce(): got = lax.all_to_all(value, axes, 0, 0, tiled=True)  50.3 us
    reduce_scatter x2, waiting for transfers between devices, body(): update = lax.psum_scatter(update, 'x', scatter_dimension=0, tiled=True)  38.2 us
    all_gather x1, waiting for transfers between devices, body(): features = lax.all_gather(acts, ('y', 'zl', 'c'), axis=1, tiled=True)  34.8 us
    dot_general x8, matrix products, dot(): lax.dot_general(a, b, (dims, ((), ())), preferred_element_type=jnp.float32)  29.8 us
    all_gather x1, waiting for transfers between devices, body(): line = lax.all_gather(line, 'x', axis=0, tiled=True)  28.5 us
    all_gather x1, waiting for transfers between devices, body(): lax.all_gather(act_line.reshape(512, 256), 'x', axis=0)  28.2 us
    all_to_all x3, starting transfers between devices, reduce(): got = lax.all_to_all(value, axes, 0, 0, tiled=True)  18.4 us
  transfers between devices with their start and end apart: 16, of which 11 were waited for; matrix products, arithmetic and copies ran while one was open for 6% of the time, Pallas kernels for 0%

profile of v3, /device:TPU:1, one launch (start us, length us, event | category | flops | bytes accessed | tf_op | source)
XLA Modules:
  0.0 388.5 jit_solution(15657266376135320125)
XLA Ops:
  9.2 3.3 collective-permute-start
  14.4 6.4 %all-to-all-start.1 = ((bf16[4,64,1792]{2,1,0:T(8,128)(2,1)}), bf16[4,64,1792]{2,1,0:T(8,128)(2,1)S(1)}, u32[]{:S(2)}, u32[]{:S(2)}) async-start(bf16[4,64,1792]{2,1,0:T(8,128)(2,1)} %broadcast_in_dim.11), calls=%async_computation.1 | async-start | bytes 1835008 | tf_op jit(solution)/shard_map/all_to_all | solution.py:39
  20.9 34.8 %all-gather.4.cloned.1.call-done = bf16[128,4096]{1,0:T(8,128)(2,1)} async-done(((bf16[128,256]{1,0:T(8,128)(2,1)}), bf16[128,4096]{1,0:T(8,128)(2,1)}) %all-gather.4.cloned.1.call-update) | async-done | bytes 1048592 | tf_op jit(solution)/shard_map/all_gather | solution.py:56
  55.6 1.7 convolution_convert_fusion.5
  59.4 6.9 %all-to-all-start = ((bf16[4,2,64,256]{3,2,1,0:T(8,128)(2,1)}), bf16[4,2,64,256]{3,2,1,0:T(8,128)(2,1)S(1)}, u32[]{:S(2)}, u32[]{:S(2)}) async-start(bf16[4,2,64,256]{3,2,1,0:T(8,128)(2,1)} %broadcast_in_dim.10), calls=%async_computation | async-start | bytes 524288 | tf_op jit(solution)/shard_map/all_to_all | solution.py:39
  66.3 2.8 constant_dynamic-update-slice_fusion.1
  69.1 2.8 constant_dynamic-update-slice_fusion
  71.9 3.5 all-to-all-done
  75.5 28.5 %all-gather.8.cloned.1.call-done = bf16[1024,1792]{1,0:T(8,128)(2,1)} async-done(((bf16[256,1792]{1,0:T(8,128)(2,1)}), bf16[1024,1792]{1,0:T(8,128)(2,1)}) %all-gather.8.cloned.1.call-update) | async-done | bytes 3670032 | tf_op jit(solution)/shard_map/all_gather | solution.py:61
  104.0 8.3 %convolution_convert_fusion.3 = bf16[1024,896]{1,0:T(8,128)(2,1)} fusion(bf16[1024,1792]{1,0:T(8,128)(2,1)} %all-gather.8.cloned.1.call-done, bf16[1792,896]{1,0:T(8,128)(2,1)} %constant_dynamic-update-slice_fusion), kind=kOutput, calls=%fused_computation.13 | convolution fusion | flops 3289251840 | bytes 8716288 | tf_op jit(solution)/shard_map/dot_general | solution.py:30
  112.3 5.0 %all-to-all-start.2 = ((bf16[8,128,896]{2,1,0:T(8,128)(2,1)}), bf16[8,128,896]{2,1,0:T(8,128)(2,1)}, u32[]{:S(2)}, u32[]{:S(2)}) async-start(bf16[8,128,896]{2,1,0:T(8,128)(2,1)} %bitcast.49), calls=%async_computation.2 | async-start | bytes 3670016 | tf_op jit(solution)/shard_map/all_to_all | solution.py:43
  118.1 28.2 %all-gather.6.cloned.1.call-done = bf16[4,512,256]{2,1,0:T(8,128)(2,1)} async-done(((bf16[1,512,256]{2,1,0:T(8,128)(2,1)}), bf16[4,512,256]{2,1,0:T(8,128)(2,1)}) %all-gather.6.cloned.1.call-update) | async-done | bytes 1048592 | tf_op jit(solution)/shard_map/all_gather | solution.py:62
  146.3 1.3 copy.11
  147.6 1.8 reduce_sum.54
  149.7 27.1 %all_to_all.70 = bf16[8,128,896]{2,1,0:T(8,128)(2,1)S(1)} all-to-all(bf16[8,128,896]{2,1,0:T(8,128)(2,1)S(1)} %broadcast_in_dim.12), channel_id=1, replica_groups=mesh['x'=4,'zh'=4,'y'=4,'zl'=2,'c'=2] {'y','zl'}, dimensions={0} | all-to-all | bytes 3670016 | tf_op jit(solution)/shard_map/all_to_all | solution.py:39
  176.8 2.8 collective-permute-start.2
  180.6 2.3 collective-permute-done.2
  183.0 1.3 fusion.9
  186.2 1.3 collective-permute-done.4
  187.5 1.5 convolution_convert_fusion.1
  189.1 30.8 %all_to_all.71 = bf16[8,160,896]{2,1,0:T(8,128)(2,1)S(1)} all-to-all(bf16[8,160,896]{2,1,0:T(8,128)(2,1)S(1)} %bitcast.47), channel_id=1, replica_groups=mesh['x'=4,'zh'=4,'y'=4,'zl'=2,'c'=2] {'y','zl'}, dimensions={0} | all-to-all | bytes 4587520 | tf_op jit(solution)/shard_map/all_to_all | solution.py:43
  222.1 30.6 %all_to_all.72 = bf16[8,160,896]{2,1,0:T(8,128)(2,1)S(1)} all-to-all(bf16[8,160,896]{2,1,0:T(8,128)(2,1)S(1)} %broadcast_in_dim.13), channel_id=1, replica_groups=mesh['x'=4,'zh'=4,'y'=4,'zl'=2,'c'=2] {'y','zl'}, dimensions={0} | all-to-all | bytes 4587520 | tf_op jit(solution)/shard_map/all_to_all | solution.py:39
  252.8 8.5 %convolution_convert_fusion = bf16[1280,1792]{1,0:T(8,128)(2,1)} fusion(bf16[1280,896]{1,0:T(8,128)(2,1)S(1)} %bitcast.48, bf16[1792,896]{1,0:T(8,128)(2,1)} %constant_dynamic-update-slice_fusion), kind=kOutput, calls=%fused_computation | convolution fusion | flops 4112711680 | bytes 10092544 | tf_op jit(solution)/shard_map/dot_general | solution.py:30
  263.8 19.5 %all_to_all.73 = bf16[8,96,896]{2,1,0:T(8,128)(2,1)S(1)} all-to-all(bf16[8,96,896]{2,1,0:T(8,128)(2,1)S(1)} %bitcast.53), channel_id=1, replica_groups=mesh['x'=4,'zh'=4,'y'=4,'zl'=2,'c'=2] {'y','zl'}, dimensions={0} | all-to-all | bytes 2752512 | tf_op jit(solution)/shard_map/all_to_all | solution.py:43
  283.6 18.3 %all_to_all.74 = bf16[8,96,896]{2,1,0:T(8,128)(2,1)S(1)} all-to-all(bf16[8,96,896]{2,1,0:T(8,128)(2,1)S(1)} %broadcast_in_dim.14), channel_id=1, replica_groups=mesh['x'=4,'zh'=4,'y'=4,'zl'=2,'c'=2] {'y','zl'}, dimensions={0} | all-to-all | bytes 2752512 | tf_op jit(solution)/shard_map/all_to_all | solution.py:39
  301.9 6.3 %convolution_convert_fusion.2 = bf16[768,1792]{1,0:T(8,128)(2,1)} fusion(bf16[768,896]{1,0:T(8,128)(2,1)S(1)} %bitcast.54, bf16[1792,896]{1,0:T(8,128)(2,1)} %constant_dynamic-update-slice_fusion), kind=kOutput, calls=%fused_computation.7 | convolution fusion | flops 2467627008 | bytes 7340032 | tf_op jit(solution)/shard_map/dot_general | solution.py:30
  308.2 5.1 %reduce-scatter.3.cloned.1.call-done = bf16[320,1792]{1,0:T(8,128)(2,1)} async-done(((bf16[1280,1792]{1,0:T(8,128)(2,1)}), bf16[320,1792]{1,0:T(8,128)(2,1)}) %reduce-scatter.3.cloned.1.call-update) | async-done | bytes 1146896 | tf_op jit(solution)/shard_map/reduce_scatter | solution.py:89
  313.3 6.7 %all-to-all-start.6 = ((bf16[4,80,1792]{2,1,0:T(8,128)(2,1)}), bf16[4,80,1792]{2,1,0:T(8,128)(2,1)S(1)}, u32[]{:S(2)}, u32[]{:S(2)}) async-start(bf16[4,80,1792]{2,1,0:T(8,128)(2,1)} %bitcast.56), calls=%async_computation.7 | async-start | bytes 2293760 | tf_op jit(solution)/shard_map/all_to_all | solution.py:43
  320.0 33.1 %reduce-scatter.5.cloned.1.call-done = bf16[192,1792]{1,0:T(8,128)(2,1)} async-done(((bf16[768,1792]{1,0:T(8,128)(2,1)}), bf16[192,1792]{1,0:T(8,128)(2,1)}) %reduce-scatter.5.cloned.1.call-update) | async-done | bytes 688144 | tf_op jit(solution)/shard_map/reduce_scatter | solution.py:89
  353.1 6.7 %all-to-all-start.9 = ((bf16[4,48,1792]{2,1,0:T(8,128)(2,1)}), bf16[4,48,1792]{2,1,0:T(8,128)(2,1)S(1)}, u32[]{:S(2)}, u32[]{:S(2)}) async-start(bf16[4,48,1792]{2,1,0:T(8,128)(2,1)} %bitcast.62), calls=%async_computation.11 | async-start | bytes 1376256 | tf_op jit(solution)/shard_map/all_to_all | solution.py:43
  360.0 17.6 %all-to-all-done.9 = bf16[4,48,1792]{2,1,0:T(8,128)(2,1)S(1)} async-done(((bf16[4,48,1792]{2,1,0:T(8,128)(2,1)}), bf16[4,48,1792]{2,1,0:T(8,128)(2,1)S(1)}, u32[]{:S(2)}, u32[]{:S(2)}) %all-to-all-start.9) | async-done | bytes 688160 | tf_op jit(solution)/shard_map/all_to_all | solution.py:43
  377.8 2.0 collective-permute-start.5
  (65 shorter events, 17.5 us)
Async XLA Ops:
  7.2 48.5 %all-gather.4.cloned.1.call-start = ((), (), s32[]{:S(2)}) async-start(), calls=%async_computation.12 | async-start | bytes 1114112 | tf_op jit(solution)/shard_map/all_gather | solution.py:56
  7.9 47.7 %copy-start = (bf16[4096,256]{1,0:T(8,128)(2,1)S(1)}, bf16[4096,256]{1,0:T(8,128)(2,1)}, u32[]{:S(2)}) copy-start(bf16[4096,256]{1,0:T(8,128)(2,1)} %param.7) | copy-start | bytes 6291460
  9.2 4.3 %collective-permute-start = (bf16[64,896]{1,0:T(8,128)(2,1)S(1)}, bf16[64,896]{1,0:T(8,128)(2,1)S(1)}, u32[]{:S(2)}, u32[]{:S(2)}) collective-permute-start(bf16[64,896]{1,0:T(8,128)(2,1)S(1)} %get-tuple-element.15), channel_id=1, source_target_pairs={{0,1},{1,0},{2,3},{3,2},{4,5},{5,4},{6,7},{7,6},{8,9},{9,8},{10,11... | collective-permute-start | bytes 344072 | tf_op jit(solution)/shard_map/ppermute | solution.py:16
  14.4 42.9 %all-to-all-start.1 = ((bf16[4,64,1792]{2,1,0:T(8,128)(2,1)}), bf16[4,64,1792]{2,1,0:T(8,128)(2,1)S(1)}, u32[]{:S(2)}, u32[]{:S(2)}) async-start(bf16[4,64,1792]{2,1,0:T(8,128)(2,1)} %broadcast_in_dim.11), calls=%async_computation.1 | async-start | bytes 1835008 | tf_op jit(solution)/shard_map/all_to_all | solution.py:39
  20.9 83.1 %all-gather.8.cloned.1.call-start = ((), (), s32[]{:S(2)}) async-start(), calls=%async_computation.14 | async-start | bytes 4587520 | tf_op jit(solution)/shard_map/all_gather | solution.py:61
  57.4 0.9 copy-start.3
  58.3 10.7 %collective-permute-start.1 = (bf16[896,896]{1,0:T(8,128)(2,1)}, bf16[896,896]{1,0:T(8,128)(2,1)}, u32[]{:S(2)}, u32[]{:S(2)}) collective-permute-start(bf16[896,896]{1,0:T(8,128)(2,1)} %param.8), channel_id=1, source_target_pairs={{0,1},{1,0},{2,3},{3,2},{4,5},{5,4},{6,7},{7,6},{8,9},{9,8},{10,11... | collective-permute-start | bytes 4816904 | tf_op jit(solution)/shard_map/ppermute | solution.py:16
  59.4 16.1 %all-to-all-start = ((bf16[4,2,64,256]{3,2,1,0:T(8,128)(2,1)}), bf16[4,2,64,256]{3,2,1,0:T(8,128)(2,1)S(1)}, u32[]{:S(2)}, u32[]{:S(2)}) async-start(bf16[4,2,64,256]{3,2,1,0:T(8,128)(2,1)} %broadcast_in_dim.10), calls=%async_computation | async-start | bytes 524288 | tf_op jit(solution)/shard_map/all_to_all | solution.py:39
  75.5 36.8 %copy-start.4 = (bf16[4,2,64,256]{3,2,1,0:T(8,128)(2,1)}, bf16[4,2,64,256]{3,2,1,0:T(8,128)(2,1)S(1)}, u32[]{:S(2)}) copy-start(bf16[4,2,64,256]{3,2,1,0:T(8,128)(2,1)S(1)} %all-to-all-done) | copy-start | bytes 786436
  112.3 35.3 %all-to-all-start.2 = ((bf16[8,128,896]{2,1,0:T(8,128)(2,1)}), bf16[8,128,896]{2,1,0:T(8,128)(2,1)}, u32[]{:S(2)}, u32[]{:S(2)}) async-start(bf16[8,128,896]{2,1,0:T(8,128)(2,1)} %bitcast.49), calls=%async_computation.2 | async-start | bytes 3670016 | tf_op jit(solution)/shard_map/all_to_all | solution.py:43
  117.3 29.0 %all-gather.6.cloned.1.call-start = ((), (), s32[]{:S(2)}) async-start(), calls=%async_computation.13 | async-start | bytes 1310720 | tf_op jit(solution)/shard_map/all_gather | solution.py:62
  118.0 195.3 %reduce-scatter.3.cloned.1.call-start = ((), (), s32[]{:S(2)}) async-start(), calls=%async_computation.15 | async-start | bytes 5734400 | tf_op jit(solution)/shard_map/reduce_scatter | solution.py:89
  176.8 6.2 %collective-permute-start.2 = (bf16[1024,896]{1,0:T(8,128)(2,1)S(1)}, bf16[1024,896]{1,0:T(8,128)(2,1)S(1)}, u32[]{:S(2)}, u32[]{:S(2)}) collective-permute-start(bf16[1024,896]{1,0:T(8,128)(2,1)S(1)} %bitcast.50), channel_id=1, source_target_pairs={{0,1},{1,0},{2,3},{3,2},{4,5},{5,4},{6,7},{7,6},{8,9},{9,8},{10,11... | collective-permute-start | bytes 5505032 | tf_op jit(solution)/shard_map/ppermute | solution.py:16
  180.3 2.7 copy-start.9
  180.5 5.5 %collective-permute-start.3 = (bf16[16,128,256]{2,1,0:T(8,128)(2,1)S(1)}, bf16[16,128,256]{2,1,0:T(8,128)(2,1)S(1)}, u32[]{:S(2)}, u32[]{:S(2)}) collective-permute-start(bf16[16,128,256]{2,1,0:T(8,128)(2,1)S(1)} %get-tuple-element.11), channel_id=1, source_target_pairs={{0,1},{1,0},{2,3},{3,2},{4,5},{5,4},{6,7},{7,6},{8,9},{9,8},{10,11... | collective-permute-start | bytes 3145736 | tf_op jit(solution)/shard_map/ppermute | solution.py:16
  184.3 1.3 copy-start.10
  185.6 3.5 copy-start.5
  185.6 1.9 collective-permute-start.4
  186.1 3.0 copy-start.1
  187.5 1.6 copy-start.7
  261.3 1.2 copy-start.2
  261.3 1.3 copy-start.6
  261.3 1.4 copy-start.8
  261.3 91.8 %reduce-scatter.5.cloned.1.call-start = ((), (), s32[]{:S(2)}) async-start(), calls=%async_computation.16 | async-start | bytes 3440640 | tf_op jit(solution)/shard_map/reduce_scatter | solution.py:89
  313.3 39.8 %all-to-all-start.6 = ((bf16[4,80,1792]{2,1,0:T(8,128)(2,1)}), bf16[4,80,1792]{2,1,0:T(8,128)(2,1)S(1)}, u32[]{:S(2)}, u32[]{:S(2)}) async-start(bf16[4,80,1792]{2,1,0:T(8,128)(2,1)} %bitcast.56), calls=%async_computation.7 | async-start | bytes 2293760 | tf_op jit(solution)/shard_map/all_to_all | solution.py:43
  353.1 24.4 %all-to-all-start.9 = ((bf16[4,48,1792]{2,1,0:T(8,128)(2,1)}), bf16[4,48,1792]{2,1,0:T(8,128)(2,1)S(1)}, u32[]{:S(2)}, u32[]{:S(2)}) async-start(bf16[4,48,1792]{2,1,0:T(8,128)(2,1)} %bitcast.62), calls=%async_computation.11 | async-start | bytes 1376256 | tf_op jit(solution)/shard_map/all_to_all | solution.py:43
  377.8 3.1 collective-permute-start.5
Sparse Core Ops, SparseCore 0:
  9.8 45.8 all-gather.3
  58.4 45.5 all-gather.7
  120.5 25.7 all-gather.5
  261.4 51.8 reduce-scatter.2
  315.7 37.3 reduce-scatter.4

commit v4 on v3

--- a/solution.py
+++ b/solution.py
@@ -53,12 +53,12 @@
     grads_chip = jnp.concatenate([halves[0], swap(halves[1])], 1)
     out_chip = jnp.concatenate([basis_out, swap(basis_out)], 0)
 
-    features = lax.all_gather(acts, ("y", "zl", "c"), axis=1, tiled=True)
-    act_local = roll(dot(features, basis_in).astype(bf16).reshape(2, 64, 256), c, 0)
-    act_line = gather(act_local, ("zh",))
+    line = gather(grads_chip, ("zh",)).reshape(256, 1792)
+    features = gather(after(acts, line), ("y", "zl", "c"))
+    line = lax.all_gather(line, "x", axis=0, tiled=True)
 
-    line = after(gather(grads_chip, ("zh",)), act_local).reshape(256, 1792)
-    line = lax.all_gather(line, "x", axis=0, tiled=True)
+    act_local = dot(features, basis_in.reshape(16, 256, 256), ((0, 2), (0, 1))).astype(bf16)
+    act_line = gather(roll(act_local.reshape(2, 64, 256), c, 0), ("zh",))
     act_proj = lax.all_gather(act_line.reshape(512, 256), "x", axis=0).reshape(4, 4, 2, 64, 256)
     act_proj = jnp.transpose(act_proj, (2, 0, 1, 3, 4)).reshape(2048, 256)
 

time: 389 us -> 374 us (0.961)
  waiting for transfers between devices: 158 us -> 118 us
  blocking collectives: 126 us -> 156 us
    all_gather x1 -> x0, waiting for transfers between devices: 34.8 us -> none  [body(): features = lax.all_gather(acts, ('y', 'zl', 'c'), axis=1, tiled=True)]
    all_to_all x3 -> x4, blocking collectives: 76 us -> 105 us  [gather(): return lax.all_to_all(copies, axes, 0, 0, tiled=True)]
    all_gather x1, waiting for transfers between devices: 28.5 us -> 8.65 us  [body(): line = lax.all_gather(line, 'x', axis=0, tiled=True)]
    all_to_all x2, waiting for transfers between devices: 3.55 us -> 18.5 us  [gather(): return lax.all_to_all(copies, axes, 0, 0, tiled=True)]
  transfers between devices with their start and end apart: 16 -> 15, of which waited for: 11 -> 11; matrix products, arithmetic and copies ran while one was open for 6% -> 6% of each run, Pallas kernels for 0% -> 0%
where the time goes in v4:
time: 374 us; the launch traced here: 373 us
  blocking collectives  156 us (42%)
  waiting for transfers between devices  118 us (32%)
  starting transfers between devices  38.7 us (10%)
  matrix products  28.6 us (8%)
  between operations  14 us (4%)
  local copies, waits for them, and re-layouts  11.8 us (3%)
  other arithmetic  6.62 us (2%)
    all_to_all x4, blocking collectives, gather(): return lax.all_to_all(copies, axes, 0, 0, tiled=True)  105 us
    all_to_all x2, blocking collectives, reduce(): got = lax.all_to_all(value, axes, 0, 0, tiled=True)  50.3 us
    reduce_scatter x2, waiting for transfers between devices, body(): update = lax.psum_scatter(update, 'x', scatter_dimension=0, tiled=True)  38.2 us
    dot_general x8, matrix products, dot(): lax.dot_general(a, b, (dims, ((), ())), preferred_element_type=jnp.float32)  28.6 us
    all_gather x1, waiting for transfers between devices, body(): lax.all_gather(act_line.reshape(512, 256), 'x', axis=0)  28.2 us
    all_to_all x2, waiting for transfers between devices, gather(): return lax.all_to_all(copies, axes, 0, 0, tiled=True)  18.5 us
    all_to_all x3, starting transfers between devices, reduce(): got = lax.all_to_all(value, axes, 0, 0, tiled=True)  18.4 us
    all_to_all x3, waiting for transfers between devices, reduce(): got = lax.all_to_all(value, axes, 0, 0, tiled=True)  17.7 us
  transfers between devices with their start and end apart: 15, of which 11 were waited for; matrix products, arithmetic and copies ran while one was open for 6% of the time, Pallas kernels for 0%

profile of v4, /device:TPU:1, one launch (start us, length us, event | category | flops | bytes accessed | tf_op | source)
XLA Modules:
  0.0 373.0 jit_solution(10160262195969540718)
XLA Ops:
  8.3 3.3 collective-permute-start
  12.7 29.2 %all_to_all.75 = bf16[4,64,1792]{2,1,0:T(8,128)(2,1)} all-to-all(bf16[4,64,1792]{2,1,0:T(8,128)(2,1)S(1)} %broadcast_in_dim.12), channel_id=1, replica_groups=mesh['x'=4,'zh'=4,'y'=4,'zl'=2,'c'=2] {'zh'}, dimensions={0} | all-to-all | bytes 1835008 | tf_op jit(solution)/shard_map/all_to_all | solution.py:39
  43.0 7.8 %all-to-all-start.1 = ((bf16[16,128,256]{2,1,0:T(8,128)(2,1)}), bf16[16,128,256]{2,1,0:T(8,128)(2,1)S(1)}, u32[]{:S(2)}, u32[]{:S(2)}) async-start(bf16[16,128,256]{2,1,0:T(8,128)(2,1)} %broadcast_in_dim.13), calls=%async_computation.1 | async-start | bytes 2097152 | tf_op jit(solution)/shard_map/all_to_all | solution.py:39
  51.0 15.6 %all-to-all-done.1 = bf16[16,128,256]{2,1,0:T(8,128)(2,1)S(1)} async-done(((bf16[16,128,256]{2,1,0:T(8,128)(2,1)}), bf16[16,128,256]{2,1,0:T(8,128)(2,1)S(1)}, u32[]{:S(2)}, u32[]{:S(2)}) %all-to-all-start.1) | async-done | bytes 1048608 | tf_op jit(solution)/shard_map/all_to_all | solution.py:39
  67.8 3.4 all-to-all-start.2
  71.3 2.8 constant_dynamic-update-slice_fusion.1
  74.0 2.7 constant_dynamic-update-slice_fusion
  76.8 2.8 all-to-all-done.2
  79.6 8.7 %all-gather.5.cloned.1.call-done = bf16[1024,1792]{1,0:T(8,128)(2,1)} async-done(((bf16[256,1792]{1,0:T(8,128)(2,1)}), bf16[1024,1792]{1,0:T(8,128)(2,1)}) %all-gather.5.cloned.1.call-update) | async-done | bytes 3670032 | tf_op jit(solution)/shard_map/all_gather | solution.py:58
  88.2 8.3 %convolution_convert_fusion.3 = bf16[1024,896]{1,0:T(8,128)(2,1)} fusion(bf16[1024,1792]{1,0:T(8,128)(2,1)} %all-gather.5.cloned.1.call-done, bf16[1792,896]{1,0:T(8,128)(2,1)} %constant_dynamic-update-slice_fusion), kind=kOutput, calls=%fused_computation.13 | convolution fusion | flops 3289251840 | bytes 8716288 | tf_op jit(solution)/shard_map/dot_general | solution.py:30
  96.5 5.0 %all-to-all-start.3 = ((bf16[8,128,896]{2,1,0:T(8,128)(2,1)}), bf16[8,128,896]{2,1,0:T(8,128)(2,1)}, u32[]{:S(2)}, u32[]{:S(2)}) async-start(bf16[8,128,896]{2,1,0:T(8,128)(2,1)} %bitcast.55), calls=%async_computation.3 | async-start | bytes 3670016 | tf_op jit(solution)/shard_map/all_to_all | solution.py:43
  102.3 28.2 %all-gather.3.cloned.1.call-done = bf16[4,512,256]{2,1,0:T(8,128)(2,1)} async-done(((bf16[1,512,256]{2,1,0:T(8,128)(2,1)}), bf16[4,512,256]{2,1,0:T(8,128)(2,1)}) %all-gather.3.cloned.1.call-update) | async-done | bytes 1048592 | tf_op jit(solution)/shard_map/all_gather | solution.py:62
  130.6 1.3 copy.11
  131.9 1.8 reduce_sum.54
  133.9 27.1 %all_to_all.76 = bf16[8,128,896]{2,1,0:T(8,128)(2,1)S(1)} all-to-all(bf16[8,128,896]{2,1,0:T(8,128)(2,1)S(1)} %broadcast_in_dim.15), channel_id=1, replica_groups=mesh['x'=4,'zh'=4,'y'=4,'zl'=2,'c'=2] {'y','zl'}, dimensions={0} | all-to-all | bytes 3670016 | tf_op jit(solution)/shard_map/all_to_all | solution.py:39
  161.0 2.8 collective-permute-start.2
  164.9 2.3 collective-permute-done.2
  167.2 1.3 fusion.9
  170.4 1.3 collective-permute-done.4
  171.8 1.5 convolution_convert_fusion.1
  173.3 30.8 %all_to_all.77 = bf16[8,160,896]{2,1,0:T(8,128)(2,1)S(1)} all-to-all(bf16[8,160,896]{2,1,0:T(8,128)(2,1)S(1)} %bitcast.53), channel_id=1, replica_groups=mesh['x'=4,'zh'=4,'y'=4,'zl'=2,'c'=2] {'y','zl'}, dimensions={0} | all-to-all | bytes 4587520 | tf_op jit(solution)/shard_map/all_to_all | solution.py:43
  206.4 30.6 %all_to_all.78 = bf16[8,160,896]{2,1,0:T(8,128)(2,1)S(1)} all-to-all(bf16[8,160,896]{2,1,0:T(8,128)(2,1)S(1)} %broadcast_in_dim.16), channel_id=1, replica_groups=mesh['x'=4,'zh'=4,'y'=4,'zl'=2,'c'=2] {'y','zl'}, dimensions={0} | all-to-all | bytes 4587520 | tf_op jit(solution)/shard_map/all_to_all | solution.py:39
  237.0 8.5 %convolution_convert_fusion = bf16[1280,1792]{1,0:T(8,128)(2,1)} fusion(bf16[1280,896]{1,0:T(8,128)(2,1)S(1)} %bitcast.54, bf16[1792,896]{1,0:T(8,128)(2,1)} %constant_dynamic-update-slice_fusion), kind=kOutput, calls=%fused_computation | convolution fusion | flops 4112711680 | bytes 10092544 | tf_op jit(solution)/shard_map/dot_general | solution.py:30
  248.0 19.5 %all_to_all.79 = bf16[8,96,896]{2,1,0:T(8,128)(2,1)S(1)} all-to-all(bf16[8,96,896]{2,1,0:T(8,128)(2,1)S(1)} %bitcast.59), channel_id=1, replica_groups=mesh['x'=4,'zh'=4,'y'=4,'zl'=2,'c'=2] {'y','zl'}, dimensions={0} | all-to-all | bytes 2752512 | tf_op jit(solution)/shard_map/all_to_all | solution.py:43
  267.8 18.3 %all_to_all.80 = bf16[8,96,896]{2,1,0:T(8,128)(2,1)S(1)} all-to-all(bf16[8,96,896]{2,1,0:T(8,128)(2,1)S(1)} %broadcast_in_dim.17), channel_id=1, replica_groups=mesh['x'=4,'zh'=4,'y'=4,'zl'=2,'c'=2] {'y','zl'}, dimensions={0} | all-to-all | bytes 2752512 | tf_op jit(solution)/shard_map/all_to_all | solution.py:39
  286.1 6.2 %convolution_convert_fusion.2 = bf16[768,1792]{1,0:T(8,128)(2,1)} fusion(bf16[768,896]{1,0:T(8,128)(2,1)S(1)} %bitcast.60, bf16[1792,896]{1,0:T(8,128)(2,1)} %constant_dynamic-update-slice_fusion), kind=kOutput, calls=%fused_computation.7 | convolution fusion | flops 2467627008 | bytes 7340032 | tf_op jit(solution)/shard_map/dot_general | solution.py:30
  292.4 5.2 %reduce-scatter.3.cloned.1.call-done = bf16[320,1792]{1,0:T(8,128)(2,1)} async-done(((bf16[1280,1792]{1,0:T(8,128)(2,1)}), bf16[320,1792]{1,0:T(8,128)(2,1)}) %reduce-scatter.3.cloned.1.call-update) | async-done | bytes 1146896 | tf_op jit(solution)/shard_map/reduce_scatter | solution.py:89
  297.5 6.7 %all-to-all-start.7 = ((bf16[4,80,1792]{2,1,0:T(8,128)(2,1)}), bf16[4,80,1792]{2,1,0:T(8,128)(2,1)S(1)}, u32[]{:S(2)}, u32[]{:S(2)}) async-start(bf16[4,80,1792]{2,1,0:T(8,128)(2,1)} %bitcast.62), calls=%async_computation.8 | async-start | bytes 2293760 | tf_op jit(solution)/shard_map/all_to_all | solution.py:43
  304.3 33.1 %reduce-scatter.5.cloned.1.call-done = bf16[192,1792]{1,0:T(8,128)(2,1)} async-done(((bf16[768,1792]{1,0:T(8,128)(2,1)}), bf16[192,1792]{1,0:T(8,128)(2,1)}) %reduce-scatter.5.cloned.1.call-update) | async-done | bytes 688144 | tf_op jit(solution)/shard_map/reduce_scatter | solution.py:89
  337.3 6.7 %all-to-all-start.10 = ((bf16[4,48,1792]{2,1,0:T(8,128)(2,1)}), bf16[4,48,1792]{2,1,0:T(8,128)(2,1)S(1)}, u32[]{:S(2)}, u32[]{:S(2)}) async-start(bf16[4,48,1792]{2,1,0:T(8,128)(2,1)} %bitcast.68), calls=%async_computation.12 | async-start | bytes 1376256 | tf_op jit(solution)/shard_map/all_to_all | solution.py:43
  344.2 17.7 %all-to-all-done.10 = bf16[4,48,1792]{2,1,0:T(8,128)(2,1)S(1)} async-done(((bf16[4,48,1792]{2,1,0:T(8,128)(2,1)}), bf16[4,48,1792]{2,1,0:T(8,128)(2,1)S(1)}, u32[]{:S(2)}, u32[]{:S(2)}) %all-to-all-start.10) | async-done | bytes 688160 | tf_op jit(solution)/shard_map/all_to_all | solution.py:43
  362.2 2.1 collective-permute-start.5
  (64 shorter events, 16.2 us)
Async XLA Ops:
  7.2 81.1 %all-gather.5.cloned.1.call-start = ((), (), s32[]{:S(2)}) async-start(), calls=%async_computation.14 | async-start | bytes 4587520 | tf_op jit(solution)/shard_map/all_gather | solution.py:58
  8.3 4.3 %collective-permute-start = (bf16[64,896]{1,0:T(8,128)(2,1)S(1)}, bf16[64,896]{1,0:T(8,128)(2,1)S(1)}, u32[]{:S(2)}, u32[]{:S(2)}) collective-permute-start(bf16[64,896]{1,0:T(8,128)(2,1)S(1)} %get-tuple-element.15), channel_id=1, source_target_pairs={{0,1},{1,0},{2,3},{3,2},{4,5},{5,4},{6,7},{7,6},{8,9},{9,8},{10,11... | collective-permute-start | bytes 344072 | tf_op jit(solution)/shard_map/ppermute | solution.py:16
  12.6 29.3 %copy-start.8 = (bf16[128,256]{1,0:T(8,128)(2,1)S(1)}, bf16[128,256]{1,0:T(8,128)(2,1)}, u32[]{:S(2)}) copy-start(bf16[128,256]{1,0:T(8,128)(2,1)} %param.5) | copy-start | bytes 196612
  41.9 24.7 %copy-start = (bf16[4096,256]{1,0:T(8,128)(2,1)S(1)}, bf16[4096,256]{1,0:T(8,128)(2,1)}, u32[]{:S(2)}) copy-start(bf16[4096,256]{1,0:T(8,128)(2,1)} %param.7) | copy-start | bytes 6291460
  43.0 23.6 %all-to-all-start.1 = ((bf16[16,128,256]{2,1,0:T(8,128)(2,1)}), bf16[16,128,256]{2,1,0:T(8,128)(2,1)S(1)}, u32[]{:S(2)}, u32[]{:S(2)}) async-start(bf16[16,128,256]{2,1,0:T(8,128)(2,1)} %broadcast_in_dim.13), calls=%async_computation.1 | async-start | bytes 2097152 | tf_op jit(solution)/shard_map/all_to_all | solution.py:39
  50.8 23.2 %collective-permute-start.1 = (bf16[896,896]{1,0:T(8,128)(2,1)}, bf16[896,896]{1,0:T(8,128)(2,1)}, u32[]{:S(2)}, u32[]{:S(2)}) collective-permute-start(bf16[896,896]{1,0:T(8,128)(2,1)} %param.8), channel_id=1, source_target_pairs={{0,1},{1,0},{2,3},{3,2},{4,5},{5,4},{6,7},{7,6},{8,9},{9,8},{10,11... | collective-permute-start | bytes 4816904 | tf_op jit(solution)/shard_map/ppermute | solution.py:16
  67.8 11.7 %all-to-all-start.2 = ((bf16[4,2,64,256]{3,2,1,0:T(8,128)(2,1)}), bf16[4,2,64,256]{3,2,1,0:T(8,128)(2,1)S(1)}, u32[]{:S(2)}, u32[]{:S(2)}) async-start(bf16[4,2,64,256]{3,2,1,0:T(8,128)(2,1)} %broadcast_in_dim.14), calls=%async_computation.2 | async-start | bytes 524288 | tf_op jit(solution)/shard_map/all_to_all | solution.py:39
  79.6 17.0 %copy-start.3 = (bf16[4,2,64,256]{3,2,1,0:T(8,128)(2,1)}, bf16[4,2,64,256]{3,2,1,0:T(8,128)(2,1)S(1)}, u32[]{:S(2)}) copy-start(bf16[4,2,64,256]{3,2,1,0:T(8,128)(2,1)S(1)} %all-to-all-done.2) | copy-start | bytes 786436
  96.5 35.3 %all-to-all-start.3 = ((bf16[8,128,896]{2,1,0:T(8,128)(2,1)}), bf16[8,128,896]{2,1,0:T(8,128)(2,1)}, u32[]{:S(2)}, u32[]{:S(2)}) async-start(bf16[8,128,896]{2,1,0:T(8,128)(2,1)} %bitcast.55), calls=%async_computation.3 | async-start | bytes 3670016 | tf_op jit(solution)/shard_map/all_to_all | solution.py:43
  101.5 29.0 %all-gather.3.cloned.1.call-start = ((), (), s32[]{:S(2)}) async-start(), calls=%async_computation.13 | async-start | bytes 1310720 | tf_op jit(solution)/shard_map/all_gather | solution.py:62
  102.3 195.3 %reduce-scatter.3.cloned.1.call-start = ((), (), s32[]{:S(2)}) async-start(), calls=%async_computation.15 | async-start | bytes 5734400 | tf_op jit(solution)/shard_map/reduce_scatter | solution.py:89
  161.0 6.2 %collective-permute-start.2 = (bf16[1024,896]{1,0:T(8,128)(2,1)S(1)}, bf16[1024,896]{1,0:T(8,128)(2,1)S(1)}, u32[]{:S(2)}, u32[]{:S(2)}) collective-permute-start(bf16[1024,896]{1,0:T(8,128)(2,1)S(1)} %bitcast.56), channel_id=1, source_target_pairs={{0,1},{1,0},{2,3},{3,2},{4,5},{5,4},{6,7},{7,6},{8,9},{9,8},{10,11... | collective-permute-start | bytes 5505032 | tf_op jit(solution)/shard_map/ppermute | solution.py:16
  164.5 2.7 copy-start.9
  164.8 5.5 %collective-permute-start.3 = (bf16[16,128,256]{2,1,0:T(8,128)(2,1)S(1)}, bf16[16,128,256]{2,1,0:T(8,128)(2,1)S(1)}, u32[]{:S(2)}, u32[]{:S(2)}) collective-permute-start(bf16[16,128,256]{2,1,0:T(8,128)(2,1)S(1)} %get-tuple-element.11), channel_id=1, source_target_pairs={{0,1},{1,0},{2,3},{3,2},{4,5},{5,4},{6,7},{7,6},{8,9},{9,8},{10,11... | collective-permute-start | bytes 3145736 | tf_op jit(solution)/shard_map/ppermute | solution.py:16
  168.5 1.3 copy-start.10
  169.8 3.5 copy-start.4
  169.8 1.9 collective-permute-start.4
  170.3 3.0 copy-start.1
  171.8 1.6 copy-start.6
  245.5 1.2 copy-start.2
  245.5 1.3 copy-start.5
  245.5 1.4 copy-start.7
  245.6 91.8 %reduce-scatter.5.cloned.1.call-start = ((), (), s32[]{:S(2)}) async-start(), calls=%async_computation.16 | async-start | bytes 3440640 | tf_op jit(solution)/shard_map/reduce_scatter | solution.py:89
  297.5 39.8 %all-to-all-start.7 = ((bf16[4,80,1792]{2,1,0:T(8,128)(2,1)}), bf16[4,80,1792]{2,1,0:T(8,128)(2,1)S(1)}, u32[]{:S(2)}, u32[]{:S(2)}) async-start(bf16[4,80,1792]{2,1,0:T(8,128)(2,1)} %bitcast.62), calls=%async_computation.8 | async-start | bytes 2293760 | tf_op jit(solution)/shard_map/all_to_all | solution.py:43
  337.3 24.6 %all-to-all-start.10 = ((bf16[4,48,1792]{2,1,0:T(8,128)(2,1)}), bf16[4,48,1792]{2,1,0:T(8,128)(2,1)S(1)}, u32[]{:S(2)}, u32[]{:S(2)}) async-start(bf16[4,48,1792]{2,1,0:T(8,128)(2,1)} %bitcast.68), calls=%async_computation.12 | async-start | bytes 1376256 | tf_op jit(solution)/shard_map/all_to_all | solution.py:43
  362.2 3.2 collective-permute-start.5
Sparse Core Ops, SparseCore 0:
  42.0 46.1 all-gather.4
  104.8 25.7 all-gather.2
  245.7 51.8 reduce-scatter.2
  300.0 37.3 reduce-scatter.4

commit v5 on v4

--- a/solution.py
+++ b/solution.py
@@ -3,6 +3,8 @@
 import jax
 import jax.numpy as jnp
 from jax import lax
+from jax.experimental import pallas as pl
+from jax.experimental.pallas import tpu as pltpu
 from jax.sharding import Mesh, PartitionSpec as P
 
 decay_rate = 0.5
@@ -28,6 +30,29 @@
 
 def dot(a, b, dims=((1,), (0,))):
     return lax.dot_general(a, b, (dims, ((), ())), preferred_element_type=jnp.float32)
+
+
+def matmul(a, b, contract):
+    rows, depth = a.shape
+    columns = b.shape[1 - contract]
+    tile = 256 if rows % 256 == 0 else 128
+
+    def kernel(a_ref, b_ref, out_ref):
+        out_ref[...] = dot(a_ref[...], b_ref[...], ((1,), (contract,))).astype(bf16)
+
+    return pl.pallas_call(
+        kernel,
+        out_shape=jax.ShapeDtypeStruct((rows, columns), bf16),
+        grid=(rows // tile,),
+        in_specs=[pl.BlockSpec((tile, depth), lambda i: (i, 0)), pl.BlockSpec(b.shape, lambda i: (0, 0))],
+        out_specs=pl.BlockSpec((tile, columns), lambda i: (i, 0)),
+        compiler_params=pltpu.CompilerParams(vmem_limit_bytes=32 * 2**20),
+        cost_estimate=pl.CostEstimate(
+            flops=2 * rows * depth * columns,
+            bytes_accessed=2 * (rows * depth + depth * columns + rows * columns),
+            transcendentals=0,
+        ),
+    )(a, b)
 
 
 def count(axes):
@@ -62,8 +87,8 @@
     act_proj = lax.all_gather(act_line.reshape(512, 256), "x", axis=0).reshape(4, 4, 2, 64, 256)
     act_proj = jnp.transpose(act_proj, (2, 0, 1, 3, 4)).reshape(2048, 256)
 
-    piece = reduce(dot(line, after(out_chip, act_line)).astype(bf16), around)
-    grad_half = gather(after(piece, act_proj), around).reshape(1024, 896)
+    piece = reduce(matmul(line, after(out_chip, act_line), 0), around)
+    grad_half = after(gather(piece, around).reshape(1024, 896), act_proj)
     grad_proj = jnp.concatenate([grad_half, swap(grad_half)], 0)
 
     act_square = act_proj * act_proj
@@ -84,7 +109,7 @@
         begin += width
         piece = reduce(dot(rows, corrected_chip).astype(bf16), around)
         left = gather(piece, around).reshape(16 * width, 896)
-        update = dot(left, out_chip, ((1,), (1,))).astype(bf16)
+        update = matmul(left, out_chip, 1)
         corrected_chip = after(corrected_chip, update)
         update = lax.psum_scatter(update, "x", scatter_dimension=0, tiled=True)
         steps.append(reduce(update, ("zh",), jnp.float32))

time: 374 us -> 379 us (1.013)
  matrix products: 28.6 us -> 5.54 us
  Pallas kernels: 0 us -> 14.6 us
  local copies, waits for them, and re-layouts: 11.8 us -> 17 us
  other arithmetic: 6.62 us -> 11.6 us
  blocking collectives: 156 us -> 160 us
    all_to_all x2 -> x3, blocking collectives: 50.3 us -> 82 us  [reduce(): got = lax.all_to_all(value, axes, 0, 0, tiled=True)]
    all_to_all x4 -> x3, blocking collectives: 105 us -> 78.3 us  [gather(): return lax.all_to_all(copies, axes, 0, 0, tiled=True)]
    dot_general x8 -> x5, matrix products: 28.6 us -> 5.54 us  [dot(): lax.dot_general(a, b, (dims, ((), ())), preferred_element_type=jnp.float32)]
    pallas_call x0 -> x3, Pallas kernels: none -> 14.6 us  [matmul(): pl.pallas_call(kernel, out_shape=jax.ShapeDtypeStruct((rows, columns), bf...]
    all_to_all x3 -> x2, starting transfers between devices: 18.4 us -> 13.5 us  [reduce(): got = lax.all_to_all(value, axes, 0, 0, tiled=True)]
    unnamed x23 -> x30, local copies, waits for them, and re-layouts: 4.13 us -> 8.9 us
    all_to_all x2 -> x3, starting transfers between devices: 11.2 us -> 15.5 us  [gather(): return lax.all_to_all(copies, axes, 0, 0, tiled=True)]
    all_to_all x2 -> x3, waiting for transfers between devices: 18.5 us -> 20.7 us  [gather(): return lax.all_to_all(copies, axes, 0, 0, tiled=True)]
  transfers between devices with their start and end apart: 15 -> 15, of which waited for: 11 -> 10; matrix products, arithmetic and copies ran while one was open for 6% -> 5% of each run, Pallas kernels for 0% -> 1%
where the time goes in v5:
time: 379 us; the launch traced here: 378 us
  blocking collectives  160 us (42%)
  waiting for transfers between devices  118 us (31%)
  starting transfers between devices  36.7 us (10%)
  local copies, waits for them, and re-layouts  17 us (4%)
  Pallas kernels  14.6 us (4%)
  between operations  14.1 us (4%)
  other arithmetic  11.6 us (3%)
  matrix products  5.54 us (1%)
    all_to_all x3, blocking collectives, reduce(): got = lax.all_to_all(value, axes, 0, 0, tiled=True)  82 us
    all_to_all x3, blocking collectives, gather(): return lax.all_to_all(copies, axes, 0, 0, tiled=True)  78.3 us
    reduce_scatter x2, waiting for transfers between devices, body(): update = lax.psum_scatter(update, 'x', scatter_dimension=0, tiled=True)  37.7 us
    all_gather x1, waiting for transfers between devices, body(): lax.all_gather(act_line.reshape(512, 256), 'x', axis=0)  29 us
    all_to_all x3, waiting for transfers between devices, gather(): return lax.all_to_all(copies, axes, 0, 0, tiled=True)  20.7 us
    all_to_all x2, waiting for transfers between devices, reduce(): got = lax.all_to_all(value, axes, 0, 0, tiled=True)  17.7 us
    all_to_all x3, starting transfers between devices, gather(): return lax.all_to_all(copies, axes, 0, 0, tiled=True)  15.5 us
    pallas_call x3, Pallas kernels, matmul(): pl.pallas_call(kernel, out_shape=jax.ShapeDtypeStruct((rows, columns), bf...  14.6 us
  transfers between devices with their start and end apart: 15, of which 10 were waited for; matrix products, arithmetic and copies ran while one was open for 5% of the time, Pallas kernels for 1%

profile of v5, /device:TPU:1, one launch (start us, length us, event | category | flops | bytes accessed | tf_op | source)
XLA Modules:
  0.0 378.0 jit_solution(3065988299315506893)
XLA Ops:
  8.3 3.3 collective-permute-start
  12.7 29.2 %all_to_all.75 = bf16[4,64,1792]{2,1,0:T(8,128)(2,1)} all-to-all(bf16[4,64,1792]{2,1,0:T(8,128)(2,1)S(1)} %broadcast_in_dim.12), channel_id=1, replica_groups=mesh['x'=4,'zh'=4,'y'=4,'zl'=2,'c'=2] {'zh'}, dimensions={0} | all-to-all | bytes 1835008 | tf_op jit(solution)/shard_map/all_to_all | solution.py:64
  43.0 7.8 %all-to-all-start.1 = ((bf16[16,128,256]{2,1,0:T(8,128)(2,1)}), bf16[16,128,256]{2,1,0:T(8,128)(2,1)S(1)}, u32[]{:S(2)}, u32[]{:S(2)}) async-start(bf16[16,128,256]{2,1,0:T(8,128)(2,1)} %broadcast_in_dim.13), calls=%async_computation.1 | async-start | bytes 2097152 | tf_op jit(solution)/shard_map/all_to_all | solution.py:64
  51.0 15.6 %all-to-all-done.1 = bf16[16,128,256]{2,1,0:T(8,128)(2,1)S(1)} async-done(((bf16[16,128,256]{2,1,0:T(8,128)(2,1)}), bf16[16,128,256]{2,1,0:T(8,128)(2,1)S(1)}, u32[]{:S(2)}, u32[]{:S(2)}) %all-to-all-start.1) | async-done | bytes 1048608 | tf_op jit(solution)/shard_map/all_to_all | solution.py:64
  67.8 3.4 all-to-all-start.2
  71.2 1.6 constant_dynamic-update-slice_fusion.1
  72.8 1.7 constant_dynamic-update-slice_fusion.b_ref
  74.5 5.0 %all-to-all-done.2 = bf16[4,2,64,256]{3,2,1,0:T(8,128)(2,1)S(1)} async-done(((bf16[4,2,64,256]{3,2,1,0:T(8,128)(2,1)}), bf16[4,2,64,256]{3,2,1,0:T(8,128)(2,1)S(1)}, u32[]{:S(2)}, u32[]{:S(2)}) %all-to-all-start.2) | async-done | bytes 262176 | tf_op jit(solution)/shard_map/all_to_all | solution.py:64
  79.6 8.7 %all-gather.5.cloned.1.call-done.a_ref = bf16[1024,1792]{1,0:T(8,128)(2,1)} async-done(((bf16[256,1792]{1,0:T(8,128)(2,1)}), bf16[1024,1792]{1,0:T(8,128)(2,1)}) %all-gather.5.cloned.1.call-update) | async-done | bytes 3670032 | tf_op jit(solution)/shard_map/all_gather | solution.py:83
  88.2 2.0 copy-done.1
  90.3 4.5 %shard_map.68 = bf16[1024,896]{1,0:T(8,128)(2,1)S(1)} custom-call(bf16[1024,1792]{1,0:T(8,128)(2,1)S(1)} %copy-done.1, bf16[1792,896]{1,0:T(8,128)(2,1)S(1)} %constant_dynamic-update-slice_fusion.b_ref), custom_call_target="tpu_custom_call" | custom-call | flops 3288334336 | bytes 8716288 | tf_op jit(solution)/shard_map/pallas_call | solution.py:43
  94.8 28.4 %all_to_all.76 = bf16[8,128,896]{2,1,0:T(8,128)(2,1)} all-to-all(bf16[8,128,896]{2,1,0:T(8,128)(2,1)S(1)} %bitcast.46), channel_id=1, replica_groups=mesh['x'=4,'zh'=4,'y'=4,'zl'=2,'c'=2] {'y','zl'}, dimensions={0} | all-to-all | bytes 3670016 | tf_op jit(solution)/shard_map/all_to_all | solution.py:68
  123.2 1.8 reduce_sum.54
  126.4 4.3 %all-to-all-start.4 = ((bf16[8,128,896]{2,1,0:T(8,128)(2,1)}), bf16[8,128,896]{2,1,0:T(8,128)(2,1)}, u32[]{:S(2)}, u32[]{:S(2)}) async-start(bf16[8,128,896]{2,1,0:T(8,128)(2,1)} %broadcast_in_dim.15), calls=%async_computation.4 | async-start | bytes 3670016 | tf_op jit(solution)/shard_map/all_to_all | solution.py:64
  131.5 29.0 %all-gather.3.cloned.1.call-done = bf16[4,512,256]{2,1,0:T(8,128)(2,1)} async-done(((bf16[1,512,256]{2,1,0:T(8,128)(2,1)}), bf16[4,512,256]{2,1,0:T(8,128)(2,1)}) %all-gather.3.cloned.1.call-update) | async-done | bytes 1048592 | tf_op jit(solution)/shard_map/all_gather | solution.py:87
  160.6 2.3 copy.11
  164.5 2.3 fusion.2
  167.1 1.9 constant_dynamic-update-slice_fusion.3
  176.6 33.4 %all_to_all.77 = bf16[8,160,896]{2,1,0:T(8,128)(2,1)} all-to-all(bf16[8,160,896]{2,1,0:T(8,128)(2,1)S(1)} %bitcast.51), channel_id=1, replica_groups=mesh['x'=4,'zh'=4,'y'=4,'zl'=2,'c'=2] {'y','zl'}, dimensions={0} | all-to-all | bytes 4587520 | tf_op jit(solution)/shard_map/all_to_all | solution.py:68
  209.9 2.0 reduce_sum.55
  212.1 30.6 %all_to_all.78 = bf16[8,160,896]{2,1,0:T(8,128)(2,1)S(1)} all-to-all(bf16[8,160,896]{2,1,0:T(8,128)(2,1)S(1)} %broadcast_in_dim.16), channel_id=1, replica_groups=mesh['x'=4,'zh'=4,'y'=4,'zl'=2,'c'=2] {'y','zl'}, dimensions={0} | all-to-all | bytes 4587520 | tf_op jit(solution)/shard_map/all_to_all | solution.py:64
  242.7 5.7 %shard_map.69 = bf16[1280,1792]{1,0:T(8,128)(2,1)S(1)} custom-call(bf16[1280,896]{1,0:T(8,128)(2,1)S(1)} %bitcast.45, bf16[1792,896]{1,0:T(8,128)(2,1)S(1)} %constant_dynamic-update-slice_fusion.b_ref), custom_call_target="tpu_custom_call" | custom-call | flops 4110417920 | bytes 10092544 | tf_op jit(solution)/shard_map/pallas_call | solution.py:43
  248.5 2.1 copy-done
  253.1 20.3 %all_to_all.79 = bf16[8,96,896]{2,1,0:T(8,128)(2,1)} all-to-all(bf16[8,96,896]{2,1,0:T(8,128)(2,1)S(1)} %bitcast.52), channel_id=1, replica_groups=mesh['x'=4,'zh'=4,'y'=4,'zl'=2,'c'=2] {'y','zl'}, dimensions={0} | all-to-all | bytes 2752512 | tf_op jit(solution)/shard_map/all_to_all | solution.py:68
  275.0 18.5 %all_to_all.80 = bf16[8,96,896]{2,1,0:T(8,128)(2,1)S(1)} all-to-all(bf16[8,96,896]{2,1,0:T(8,128)(2,1)S(1)} %broadcast_in_dim.17), channel_id=1, replica_groups=mesh['x'=4,'zh'=4,'y'=4,'zl'=2,'c'=2] {'y','zl'}, dimensions={0} | all-to-all | bytes 2752512 | tf_op jit(solution)/shard_map/all_to_all | solution.py:64
  293.5 4.4 %shard_map.70 = bf16[768,1792]{1,0:T(8,128)(2,1)} custom-call(bf16[768,896]{1,0:T(8,128)(2,1)S(1)} %bitcast.47, bf16[1792,896]{1,0:T(8,128)(2,1)S(1)} %constant_dynamic-update-slice_fusion.b_ref), custom_call_target="tpu_custom_call" | custom-call | flops 2466250752 | bytes 7340032 | tf_op jit(solution)/shard_map/pallas_call | solution.py:43
  297.9 4.6 %reduce-scatter.3.cloned.1.call-done = bf16[320,1792]{1,0:T(8,128)(2,1)} async-done(((bf16[1280,1792]{1,0:T(8,128)(2,1)}), bf16[320,1792]{1,0:T(8,128)(2,1)}) %reduce-scatter.3.cloned.1.call-update) | async-done | bytes 1146896 | tf_op jit(solution)/shard_map/reduce_scatter | solution.py:114
  302.5 6.7 %all-to-all-start.7 = ((bf16[4,80,1792]{2,1,0:T(8,128)(2,1)}), bf16[4,80,1792]{2,1,0:T(8,128)(2,1)S(1)}, u32[]{:S(2)}, u32[]{:S(2)}) async-start(bf16[4,80,1792]{2,1,0:T(8,128)(2,1)} %bitcast.54), calls=%async_computation.8 | async-start | bytes 2293760 | tf_op jit(solution)/shard_map/all_to_all | solution.py:68
  309.2 33.1 %reduce-scatter.5.cloned.1.call-done = bf16[192,1792]{1,0:T(8,128)(2,1)} async-done(((bf16[768,1792]{1,0:T(8,128)(2,1)}), bf16[192,1792]{1,0:T(8,128)(2,1)}) %reduce-scatter.5.cloned.1.call-update) | async-done | bytes 688144 | tf_op jit(solution)/shard_map/reduce_scatter | solution.py:114
  342.3 6.7 %all-to-all-start.10 = ((bf16[4,48,1792]{2,1,0:T(8,128)(2,1)}), bf16[4,48,1792]{2,1,0:T(8,128)(2,1)S(1)}, u32[]{:S(2)}, u32[]{:S(2)}) async-start(bf16[4,48,1792]{2,1,0:T(8,128)(2,1)} %bitcast.60), calls=%async_computation.12 | async-start | bytes 1376256 | tf_op jit(solution)/shard_map/all_to_all | solution.py:68
  349.2 17.7 %all-to-all-done.10 = bf16[4,48,1792]{2,1,0:T(8,128)(2,1)S(1)} async-done(((bf16[4,48,1792]{2,1,0:T(8,128)(2,1)}), bf16[4,48,1792]{2,1,0:T(8,128)(2,1)S(1)}, u32[]{:S(2)}, u32[]{:S(2)}) %all-to-all-start.10) | async-done | bytes 688160 | tf_op jit(solution)/shard_map/all_to_all | solution.py:68
  367.1 2.1 collective-permute-start.5
  (72 shorter events, 23.2 us)
Async XLA Ops:
  7.2 81.1 %all-gather.5.cloned.1.call-start = ((), (), s32[]{:S(2)}) async-start(), calls=%async_computation.14 | async-start | bytes 4587520 | tf_op jit(solution)/shard_map/all_gather | solution.py:83
  8.3 4.3 %collective-permute-start = (bf16[64,896]{1,0:T(8,128)(2,1)S(1)}, bf16[64,896]{1,0:T(8,128)(2,1)S(1)}, u32[]{:S(2)}, u32[]{:S(2)}) collective-permute-start(bf16[64,896]{1,0:T(8,128)(2,1)S(1)} %get-tuple-element.15), channel_id=1, source_target_pairs={{0,1},{1,0},{2,3},{3,2},{4,5},{5,4},{6,7},{7,6},{8,9},{9,8},{10,11... | collective-permute-start | bytes 344072 | tf_op jit(solution)/shard_map/ppermute | solution.py:18
  12.6 29.3 %copy-start.11 = (bf16[128,256]{1,0:T(8,128)(2,1)S(1)}, bf16[128,256]{1,0:T(8,128)(2,1)}, u32[]{:S(2)}) copy-start(bf16[128,256]{1,0:T(8,128)(2,1)} %param.5) | copy-start | bytes 196612
  41.9 24.7 %copy-start.3 = (bf16[4096,256]{1,0:T(8,128)(2,1)S(1)}, bf16[4096,256]{1,0:T(8,128)(2,1)}, u32[]{:S(2)}) copy-start(bf16[4096,256]{1,0:T(8,128)(2,1)} %param.7) | copy-start | bytes 6291460
  43.0 23.6 %all-to-all-start.1 = ((bf16[16,128,256]{2,1,0:T(8,128)(2,1)}), bf16[16,128,256]{2,1,0:T(8,128)(2,1)S(1)}, u32[]{:S(2)}, u32[]{:S(2)}) async-start(bf16[16,128,256]{2,1,0:T(8,128)(2,1)} %broadcast_in_dim.13), calls=%async_computation.1 | async-start | bytes 2097152 | tf_op jit(solution)/shard_map/all_to_all | solution.py:64
  50.8 22.1 %collective-permute-start.1 = (bf16[896,896]{1,0:T(8,128)(2,1)}, bf16[896,896]{1,0:T(8,128)(2,1)}, u32[]{:S(2)}, u32[]{:S(2)}) collective-permute-start(bf16[896,896]{1,0:T(8,128)(2,1)} %param.8), channel_id=1, source_target_pairs={{0,1},{1,0},{2,3},{3,2},{4,5},{5,4},{6,7},{7,6},{8,9},{9,8},{10,11... | collective-permute-start | bytes 4816904 | tf_op jit(solution)/shard_map/ppermute | solution.py:18
  67.8 11.7 %all-to-all-start.2 = ((bf16[4,2,64,256]{3,2,1,0:T(8,128)(2,1)}), bf16[4,2,64,256]{3,2,1,0:T(8,128)(2,1)S(1)}, u32[]{:S(2)}, u32[]{:S(2)}) async-start(bf16[4,2,64,256]{3,2,1,0:T(8,128)(2,1)} %broadcast_in_dim.14), calls=%async_computation.2 | async-start | bytes 524288 | tf_op jit(solution)/shard_map/all_to_all | solution.py:64
  79.6 15.2 %copy-start.6 = (bf16[4,2,64,256]{3,2,1,0:T(8,128)(2,1)}, bf16[4,2,64,256]{3,2,1,0:T(8,128)(2,1)S(1)}, u32[]{:S(2)}) copy-start(bf16[4,2,64,256]{3,2,1,0:T(8,128)(2,1)S(1)} %all-to-all-done.2) | copy-start | bytes 786436
  88.2 2.0 copy-start.1
  126.4 36.5 %all-to-all-start.4 = ((bf16[8,128,896]{2,1,0:T(8,128)(2,1)}), bf16[8,128,896]{2,1,0:T(8,128)(2,1)}, u32[]{:S(2)}, u32[]{:S(2)}) async-start(bf16[8,128,896]{2,1,0:T(8,128)(2,1)} %broadcast_in_dim.15), calls=%async_computation.4 | async-start | bytes 3670016 | tf_op jit(solution)/shard_map/all_to_all | solution.py:64
  130.7 29.8 %all-gather.3.cloned.1.call-start = ((), (), s32[]{:S(2)}) async-start(), calls=%async_computation.13 | async-start | bytes 1310720 | tf_op jit(solution)/shard_map/all_gather | solution.py:87
  131.5 171.0 %reduce-scatter.3.cloned.1.call-start = ((), (), s32[]{:S(2)}) async-start(), calls=%async_computation.15 | async-start | bytes 5734400 | tf_op jit(solution)/shard_map/reduce_scatter | solution.py:114
  162.9 6.1 %collective-permute-start.2 = (bf16[1024,896]{1,0:T(8,128)(2,1)}, bf16[1024,896]{1,0:T(8,128)(2,1)S(1)}, u32[]{:S(2)}, u32[]{:S(2)}) collective-permute-start(bf16[1024,896]{1,0:T(8,128)(2,1)} %bitcast.12), channel_id=1, source_target_pairs={{0,1},{1,0},{2,3},{3,2},{4,5},{5,4},{6,7},{7,6},{8,9},{9,8},{10,11... | collective-permute-start | bytes 5505032 | tf_op jit(solution)/shard_map/ppermute | solution.py:18
  166.9 6.5 %copy-start.2 = (bf16[16,128,256]{2,1,0:T(8,128)(2,1)}, bf16[16,128,256]{2,1,0:T(8,128)(2,1)S(1)}, u32[]{:S(2)}) copy-start(bf16[16,128,256]{2,1,0:T(8,128)(2,1)S(1)} %get-tuple-element.10) | copy-start | bytes 3145732
  166.9 6.5 %collective-permute-start.3 = (bf16[16,128,256]{2,1,0:T(8,128)(2,1)S(1)}, bf16[16,128,256]{2,1,0:T(8,128)(2,1)S(1)}, u32[]{:S(2)}, u32[]{:S(2)}) collective-permute-start(bf16[16,128,256]{2,1,0:T(8,128)(2,1)S(1)} %get-tuple-element.11), channel_id=1, source_target_pairs={{0,1},{1,0},{2,3},{3,2},{4,5},{5,4},{6,7},{7,6},{8,9},{9,8},{10,11... | collective-permute-start | bytes 3145736 | tf_op jit(solution)/shard_map/ppermute | solution.py:18
  168.9 1.2 copy-start.5
  169.0 1.5 copy-start.12
  171.8 1.3 copy-start.13
  173.1 3.4 copy-start.7
  173.1 1.9 collective-permute-start.4
  173.4 3.1 copy-start.4
  175.0 1.5 copy-start.9
  248.4 2.1 copy-start
  250.6 91.8 %reduce-scatter.5.cloned.1.call-start = ((), (), s32[]{:S(2)}) async-start(), calls=%async_computation.16 | async-start | bytes 3440640 | tf_op jit(solution)/shard_map/reduce_scatter | solution.py:114
  250.6 1.3 copy-start.8
  250.6 1.4 copy-start.10
  302.5 39.8 %all-to-all-start.7 = ((bf16[4,80,1792]{2,1,0:T(8,128)(2,1)}), bf16[4,80,1792]{2,1,0:T(8,128)(2,1)S(1)}, u32[]{:S(2)}, u32[]{:S(2)}) async-start(bf16[4,80,1792]{2,1,0:T(8,128)(2,1)} %bitcast.54), calls=%async_computation.8 | async-start | bytes 2293760 | tf_op jit(solution)/shard_map/all_to_all | solution.py:68
  342.3 24.6 %all-to-all-start.10 = ((bf16[4,48,1792]{2,1,0:T(8,128)(2,1)}), bf16[4,48,1792]{2,1,0:T(8,128)(2,1)S(1)}, u32[]{:S(2)}, u32[]{:S(2)}) async-start(bf16[4,48,1792]{2,1,0:T(8,128)(2,1)} %bitcast.60), calls=%async_computation.12 | async-start | bytes 1376256 | tf_op jit(solution)/shard_map/all_to_all | solution.py:68
  367.1 3.2 collective-permute-start.5
Sparse Core Ops, SparseCore 0:
  42.0 46.1 all-gather.4
  134.0 26.5 all-gather.2
  250.7 51.7 reduce-scatter.2
  304.9 37.3 reduce-scatter.4

commit v6 on v5

--- a/solution.py
+++ b/solution.py
@@ -46,7 +46,7 @@
         grid=(rows // tile,),
         in_specs=[pl.BlockSpec((tile, depth), lambda i: (i, 0)), pl.BlockSpec(b.shape, lambda i: (0, 0))],
         out_specs=pl.BlockSpec((tile, columns), lambda i: (i, 0)),
-        compiler_params=pltpu.CompilerParams(vmem_limit_bytes=32 * 2**20),
+        compiler_params=pltpu.CompilerParams(vmem_limit_bytes=56 * 2**20),
         cost_estimate=pl.CostEstimate(
             flops=2 * rows * depth * columns,
             bytes_accessed=2 * (rows * depth + depth * columns + rows * columns),
@@ -83,12 +83,11 @@
     line = lax.all_gather(line, "x", axis=0, tiled=True)
 
     act_local = dot(features, basis_in.reshape(16, 256, 256), ((0, 2), (0, 1))).astype(bf16)
-    act_line = gather(roll(act_local.reshape(2, 64, 256), c, 0), ("zh",))
-    act_proj = lax.all_gather(act_line.reshape(512, 256), "x", axis=0).reshape(4, 4, 2, 64, 256)
-    act_proj = jnp.transpose(act_proj, (2, 0, 1, 3, 4)).reshape(2048, 256)
+    act_line = gather(roll(act_local.reshape(2, 64, 256), c, 0), ("x", "zh"))
+    act_proj = jnp.transpose(act_line, (1, 0, 2, 3)).reshape(2048, 256)
 
-    piece = reduce(matmul(line, after(out_chip, act_line), 0), around)
-    grad_half = after(gather(piece, around).reshape(1024, 896), act_proj)
+    piece = reduce(matmul(line, after(out_chip, act_proj), 0), around)
+    grad_half = gather(piece, around).reshape(1024, 896)
     grad_proj = jnp.concatenate([grad_half, swap(grad_half)], 0)
 
     act_square = act_proj * act_proj

time: 379 us -> 376 us (level)
  blocking collectives: 160 us -> 206 us
  waiting for transfers between devices: 118 us -> 80.4 us
  Pallas kernels: 14.6 us -> 23.7 us
  starting transfers between devices: 36.7 us -> 29.1 us
  local copies, waits for them, and re-layouts: 17 us -> 9.56 us
  other arithmetic: 11.6 us -> 6.62 us
    all_to_all x3 -> x5, blocking collectives: 78.3 us -> 126 us  [gather(): return lax.all_to_all(copies, axes, 0, 0, tiled=True)]
    all_gather x1 -> x0, waiting for transfers between devices: 29 us -> none  [body(): lax.all_gather(act_line.reshape(512, 256), 'x', axis=0)]
    all_to_all x3 -> x1, starting transfers between devices: 15.5 us -> 5.27 us  [gather(): return lax.all_to_all(copies, axes, 0, 0, tiled=True)]
    pallas_call x3, Pallas kernels: 14.6 us -> 23.7 us  [matmul(): pl.pallas_call(kernel, out_shape=jax.ShapeDtypeStruct((rows, columns), bf...]
    all_gather x1, waiting for transfers between devices: 8.66 us -> 3.67 us  [body(): line = lax.all_gather(line, 'x', axis=0, tiled=True)]
    unnamed x30 -> x23, local copies, waits for them, and re-layouts: 8.9 us -> 4.1 us
    all_to_all x3 -> x1, waiting for transfers between devices: 20.7 us -> 16.3 us  [gather(): return lax.all_to_all(copies, axes, 0, 0, tiled=True)]
  transfers between devices with their start and end apart: 15 -> 12, of which waited for: 10 -> 10; matrix products, arithmetic and copies ran while one was open for 5% -> 3% of each run, Pallas kernels for 1% -> 2%
where the time goes in v6:
time: 376 us; the launch traced here: 375 us
  blocking collectives  206 us (55%)
  waiting for transfers between devices  80.4 us (21%)
  starting transfers between devices  29.1 us (8%)
  Pallas kernels  23.7 us (6%)
  between operations  14 us (4%)
  local copies, waits for them, and re-layouts  9.56 us (3%)
  other arithmetic  6.62 us (2%)
  matrix products  5.54 us (1%)
    all_to_all x5, blocking collectives, gather(): return lax.all_to_all(copies, axes, 0, 0, tiled=True)  126 us
    all_to_all x3, blocking collectives, reduce(): got = lax.all_to_all(value, axes, 0, 0, tiled=True)  80 us
    reduce_scatter x2, waiting for transfers between devices, body(): update = lax.psum_scatter(update, 'x', scatter_dimension=0, tiled=True)  36.6 us
    pallas_call x3, Pallas kernels, matmul(): pl.pallas_call(kernel, out_shape=jax.ShapeDtypeStruct((rows, columns), bf...  23.7 us
    all_to_all x2, waiting for transfers between devices, reduce(): got = lax.all_to_all(value, axes, 0, 0, tiled=True)  17.5 us
    all_to_all x1, waiting for transfers between devices, gather(): return lax.all_to_all(copies, axes, 0, 0, tiled=True)  16.3 us
    all_to_all x2, starting transfers between devices, reduce(): got = lax.all_to_all(value, axes, 0, 0, tiled=True)  13.5 us
    ppermute x6, starting transfers between devices, swap(): return lax.ppermute(value, 'c', [(0, 1), (1, 0)])  10.2 us
  transfers between devices with their start and end apart: 12, of which 10 were waited for; matrix products, arithmetic and copies ran while one was open for 3% of the time, Pallas kernels for 2%

profile of v6, /device:TPU:1, one launch (start us, length us, event | category | flops | bytes accessed | tf_op | source)
XLA Modules:
  0.0 375.4 jit_solution(7394322165468131468)
XLA Ops:
  8.3 3.3 collective-permute-start
  12.7 29.2 %all_to_all.75 = bf16[4,64,1792]{2,1,0:T(8,128)(2,1)} all-to-all(bf16[4,64,1792]{2,1,0:T(8,128)(2,1)S(1)} %broadcast_in_dim.12), channel_id=1, replica_groups=mesh['x'=4,'zh'=4,'y'=4,'zl'=2,'c'=2] {'zh'}, dimensions={0} | all-to-all | bytes 1835008 | tf_op jit(solution)/shard_map/all_to_all | solution.py:64
  42.0 23.1 %all_to_all.76 = bf16[16,128,256]{2,1,0:T(8,128)(2,1)S(1)} all-to-all(bf16[16,128,256]{2,1,0:T(8,128)(2,1)S(1)} %broadcast_in_dim.13), channel_id=1, replica_groups=mesh['x'=4,'zh'=4,'y'=4,'zl'=2,'c'=2] {'y','zl','c'}, dimensions={0} | all-to-all | bytes 2097152 | tf_op jit(solution)/shard_map/all_to_all | solution.py:64
  65.7 1.2 broadcast_in_dim.14
  66.9 5.3 %all-to-all-start.2 = ((bf16[16,2,64,256]{3,2,1,0:T(8,128)(2,1)}), bf16[16,2,64,256]{3,2,1,0:T(8,128)(2,1)S(1)}, u32[]{:S(2)}, u32[]{:S(2)}) async-start(bf16[16,2,64,256]{3,2,1,0:T(8,128)(2,1)} %broadcast_in_dim.14), calls=%async_computation.2 | async-start | bytes 2097152 | tf_op jit(solution)/shard_map/all_to_all | solution.py:64
  72.2 1.5 collective-permute-start.1
  73.8 2.8 constant_dynamic-update-slice_fusion.1
  77.0 1.3 constant_dynamic-update-slice_fusion.b_ref
  78.3 16.3 %all-to-all-done.2 = bf16[16,2,64,256]{3,2,1,0:T(8,128)(2,1)S(1)} async-done(((bf16[16,2,64,256]{3,2,1,0:T(8,128)(2,1)}), bf16[16,2,64,256]{3,2,1,0:T(8,128)(2,1)S(1)}, u32[]{:S(2)}, u32[]{:S(2)}) %all-to-all-start.2) | async-done | bytes 1048608 | tf_op jit(solution)/shard_map/all_to_all | solution.py:64
  95.8 3.7 all-gather.2.cloned.1.call-done.a_ref
  99.4 7.7 %shard_map.68 = bf16[1024,896]{1,0:T(8,128)(2,1)} custom-call(bf16[1024,1792]{1,0:T(8,128)(2,1)} %all-gather.2.cloned.1.call-done.a_ref, bf16[1792,896]{1,0:T(8,128)(2,1)} %constant_dynamic-update-slice_fusion.b_ref), custom_call_target="tpu_custom_call" | custom-call | flops 3288334336 | bytes 8716288 | tf_op jit(solution)/shard_map/pallas_call | solution.py:43
  107.2 30.2 %all_to_all.77 = bf16[8,128,896]{2,1,0:T(8,128)(2,1)} all-to-all(bf16[8,128,896]{2,1,0:T(8,128)(2,1)} %bitcast.50), channel_id=1, replica_groups=mesh['x'=4,'zh'=4,'y'=4,'zl'=2,'c'=2] {'y','zl'}, dimensions={0} | all-to-all | bytes 3670016 | tf_op jit(solution)/shard_map/all_to_all | solution.py:68
  137.3 1.8 reduce_sum.54
  139.4 24.7 %all_to_all.78 = bf16[8,128,896]{2,1,0:T(8,128)(2,1)S(1)} all-to-all(bf16[8,128,896]{2,1,0:T(8,128)(2,1)S(1)} %broadcast_in_dim.15), channel_id=1, replica_groups=mesh['x'=4,'zh'=4,'y'=4,'zl'=2,'c'=2] {'y','zl'}, dimensions={0} | all-to-all | bytes 3670016 | tf_op jit(solution)/shard_map/all_to_all | solution.py:64
  164.0 2.9 collective-permute-start.2
  168.0 2.3 collective-permute-done.2
  170.3 1.3 fusion.9
  171.6 1.3 fusion.15
  173.5 1.3 collective-permute-done.4
  174.8 1.5 convolution_convert_fusion
  176.4 30.9 %all_to_all.79 = bf16[8,160,896]{2,1,0:T(8,128)(2,1)S(1)} all-to-all(bf16[8,160,896]{2,1,0:T(8,128)(2,1)S(1)} %bitcast.45), channel_id=1, replica_groups=mesh['x'=4,'zh'=4,'y'=4,'zl'=2,'c'=2] {'y','zl'}, dimensions={0} | all-to-all | bytes 4587520 | tf_op jit(solution)/shard_map/all_to_all | solution.py:68
  209.5 30.7 %all_to_all.80 = bf16[8,160,896]{2,1,0:T(8,128)(2,1)} all-to-all(bf16[8,160,896]{2,1,0:T(8,128)(2,1)S(1)} %broadcast_in_dim.16), channel_id=1, replica_groups=mesh['x'=4,'zh'=4,'y'=4,'zl'=2,'c'=2] {'y','zl'}, dimensions={0} | all-to-all | bytes 4587520 | tf_op jit(solution)/shard_map/all_to_all | solution.py:64
  240.1 9.2 %shard_map.69 = bf16[1280,1792]{1,0:T(8,128)(2,1)} custom-call(bf16[1280,896]{1,0:T(8,128)(2,1)} %bitcast.46, bf16[1792,896]{1,0:T(8,128)(2,1)} %constant_dynamic-update-slice_fusion.b_ref), custom_call_target="tpu_custom_call" | custom-call | flops 4110417920 | bytes 10092544 | tf_op jit(solution)/shard_map/pallas_call | solution.py:43
  251.8 19.0 %all_to_all.81 = bf16[8,96,896]{2,1,0:T(8,128)(2,1)S(1)} all-to-all(bf16[8,96,896]{2,1,0:T(8,128)(2,1)S(1)} %bitcast.51), channel_id=1, replica_groups=mesh['x'=4,'zh'=4,'y'=4,'zl'=2,'c'=2] {'y','zl'}, dimensions={0} | all-to-all | bytes 2752512 | tf_op jit(solution)/shard_map/all_to_all | solution.py:68
  271.2 18.8 %all_to_all.82 = bf16[8,96,896]{2,1,0:T(8,128)(2,1)} all-to-all(bf16[8,96,896]{2,1,0:T(8,128)(2,1)S(1)} %broadcast_in_dim.17), channel_id=1, replica_groups=mesh['x'=4,'zh'=4,'y'=4,'zl'=2,'c'=2] {'y','zl'}, dimensions={0} | all-to-all | bytes 2752512 | tf_op jit(solution)/shard_map/all_to_all | solution.py:64
  290.0 6.8 %shard_map.70 = bf16[768,1792]{1,0:T(8,128)(2,1)} custom-call(bf16[768,896]{1,0:T(8,128)(2,1)} %bitcast.52, bf16[1792,896]{1,0:T(8,128)(2,1)} %constant_dynamic-update-slice_fusion.b_ref), custom_call_target="tpu_custom_call" | custom-call | flops 2466250752 | bytes 7340032 | tf_op jit(solution)/shard_map/pallas_call | solution.py:43
  296.8 3.4 reduce-scatter.3.cloned.1.call-done
  300.1 6.7 %all-to-all-start.7 = ((bf16[4,80,1792]{2,1,0:T(8,128)(2,1)}), bf16[4,80,1792]{2,1,0:T(8,128)(2,1)S(1)}, u32[]{:S(2)}, u32[]{:S(2)}) async-start(bf16[4,80,1792]{2,1,0:T(8,128)(2,1)} %bitcast.54), calls=%async_computation.8 | async-start | bytes 2293760 | tf_op jit(solution)/shard_map/all_to_all | solution.py:68
  306.9 33.2 %reduce-scatter.5.cloned.1.call-done = bf16[192,1792]{1,0:T(8,128)(2,1)} async-done(((bf16[768,1792]{1,0:T(8,128)(2,1)}), bf16[192,1792]{1,0:T(8,128)(2,1)}) %reduce-scatter.5.cloned.1.call-update) | async-done | bytes 688144 | tf_op jit(solution)/shard_map/reduce_scatter | solution.py:113
  340.1 6.7 %all-to-all-start.10 = ((bf16[4,48,1792]{2,1,0:T(8,128)(2,1)}), bf16[4,48,1792]{2,1,0:T(8,128)(2,1)S(1)}, u32[]{:S(2)}, u32[]{:S(2)}) async-start(bf16[4,48,1792]{2,1,0:T(8,128)(2,1)} %bitcast.58), calls=%async_computation.12 | async-start | bytes 1376256 | tf_op jit(solution)/shard_map/all_to_all | solution.py:68
  346.9 17.5 %all-to-all-done.10 = bf16[4,48,1792]{2,1,0:T(8,128)(2,1)S(1)} async-done(((bf16[4,48,1792]{2,1,0:T(8,128)(2,1)}), bf16[4,48,1792]{2,1,0:T(8,128)(2,1)S(1)}, u32[]{:S(2)}, u32[]{:S(2)}) %all-to-all-start.10) | async-done | bytes 688160 | tf_op jit(solution)/shard_map/all_to_all | solution.py:68
  364.7 1.9 collective-permute-start.5
  (59 shorter events, 13.9 us)
Async XLA Ops:
  7.2 92.3 %all-gather.2.cloned.1.call-start = ((), (), s32[]{:S(2)}) async-start(), calls=%async_computation.13 | async-start | bytes 4587520 | tf_op jit(solution)/shard_map/all_gather | solution.py:83
  8.3 4.3 %collective-permute-start = (bf16[64,896]{1,0:T(8,128)(2,1)S(1)}, bf16[64,896]{1,0:T(8,128)(2,1)S(1)}, u32[]{:S(2)}, u32[]{:S(2)}) collective-permute-start(bf16[64,896]{1,0:T(8,128)(2,1)S(1)} %get-tuple-element.13), channel_id=1, source_target_pairs={{0,1},{1,0},{2,3},{3,2},{4,5},{5,4},{6,7},{7,6},{8,9},{9,8},{10,11... | collective-permute-start | bytes 344072 | tf_op jit(solution)/shard_map/ppermute | solution.py:18
  12.6 29.3 %copy-start.8 = (bf16[128,256]{1,0:T(8,128)(2,1)S(1)}, bf16[128,256]{1,0:T(8,128)(2,1)}, u32[]{:S(2)}) copy-start(bf16[128,256]{1,0:T(8,128)(2,1)} %param.5) | copy-start | bytes 196612
  41.9 23.3 %copy-start = (bf16[4096,256]{1,0:T(8,128)(2,1)S(1)}, bf16[4096,256]{1,0:T(8,128)(2,1)}, u32[]{:S(2)}) copy-start(bf16[4096,256]{1,0:T(8,128)(2,1)} %param.7) | copy-start | bytes 6291460
  66.9 27.8 %all-to-all-start.2 = ((bf16[16,2,64,256]{3,2,1,0:T(8,128)(2,1)}), bf16[16,2,64,256]{3,2,1,0:T(8,128)(2,1)S(1)}, u32[]{:S(2)}, u32[]{:S(2)}) async-start(bf16[16,2,64,256]{3,2,1,0:T(8,128)(2,1)} %broadcast_in_dim.14), calls=%async_computation.2 | async-start | bytes 2097152 | tf_op jit(solution)/shard_map/all_to_all | solution.py:64
  72.2 227.9 %reduce-scatter.3.cloned.1.call-start = ((), (), s32[]{:S(2)}) async-start(), calls=%async_computation.14 | async-start | bytes 5734400 | tf_op jit(solution)/shard_map/reduce_scatter | solution.py:113
  72.2 4.8 %collective-permute-start.1 = (bf16[896,896]{1,0:T(8,128)(2,1)}, bf16[896,896]{1,0:T(8,128)(2,1)S(1)}, u32[]{:S(2)}, u32[]{:S(2)}) collective-permute-start(bf16[896,896]{1,0:T(8,128)(2,1)} %param.8), channel_id=1, source_target_pairs={{0,1},{1,0},{2,3},{3,2},{4,5},{5,4},{6,7},{7,6},{8,9},{9,8},{10,11... | collective-permute-start | bytes 4816904 | tf_op jit(solution)/shard_map/ppermute | solution.py:18
  164.0 6.3 %collective-permute-start.2 = (bf16[1024,896]{1,0:T(8,128)(2,1)S(1)}, bf16[1024,896]{1,0:T(8,128)(2,1)S(1)}, u32[]{:S(2)}, u32[]{:S(2)}) collective-permute-start(bf16[1024,896]{1,0:T(8,128)(2,1)S(1)} %bitcast.47), channel_id=1, source_target_pairs={{0,1},{1,0},{2,3},{3,2},{4,5},{5,4},{6,7},{7,6},{8,9},{9,8},{10,11... | collective-permute-start | bytes 5505032 | tf_op jit(solution)/shard_map/ppermute | solution.py:18
  167.6 2.7 copy-start.3
  167.6 2.7 copy-start.9
  167.9 5.5 %collective-permute-start.3 = (bf16[16,128,256]{2,1,0:T(8,128)(2,1)S(1)}, bf16[16,128,256]{2,1,0:T(8,128)(2,1)S(1)}, u32[]{:S(2)}, u32[]{:S(2)}) collective-permute-start(bf16[16,128,256]{2,1,0:T(8,128)(2,1)S(1)} %get-tuple-element.9), channel_id=1, source_target_pairs={{0,1},{1,0},{2,3},{3,2},{4,5},{5,4},{6,7},{7,6},{8,9},{9,8},{10,11... | collective-permute-start | bytes 3145736 | tf_op jit(solution)/shard_map/ppermute | solution.py:18
  171.6 1.3 copy-start.10
  172.9 3.5 copy-start.4
  172.9 1.9 collective-permute-start.4
  173.4 3.0 copy-start.1
  174.8 1.6 copy-start.6
  249.3 1.2 copy-start.2
  249.3 1.3 copy-start.5
  249.3 1.4 copy-start.7
  249.4 90.7 %reduce-scatter.5.cloned.1.call-start = ((), (), s32[]{:S(2)}) async-start(), calls=%async_computation.15 | async-start | bytes 3440640 | tf_op jit(solution)/shard_map/reduce_scatter | solution.py:113
  300.1 40.0 %all-to-all-start.7 = ((bf16[4,80,1792]{2,1,0:T(8,128)(2,1)}), bf16[4,80,1792]{2,1,0:T(8,128)(2,1)S(1)}, u32[]{:S(2)}, u32[]{:S(2)}) async-start(bf16[4,80,1792]{2,1,0:T(8,128)(2,1)} %bitcast.54), calls=%async_computation.8 | async-start | bytes 2293760 | tf_op jit(solution)/shard_map/all_to_all | solution.py:68
  340.1 24.4 %all-to-all-start.10 = ((bf16[4,48,1792]{2,1,0:T(8,128)(2,1)}), bf16[4,48,1792]{2,1,0:T(8,128)(2,1)S(1)}, u32[]{:S(2)}, u32[]{:S(2)}) async-start(bf16[4,48,1792]{2,1,0:T(8,128)(2,1)} %bitcast.58), calls=%async_computation.12 | async-start | bytes 1376256 | tf_op jit(solution)/shard_map/all_to_all | solution.py:68
  364.7 3.1 collective-permute-start.5
Sparse Core Ops, SparseCore 0:
  42.0 57.3 all-gather.1
  249.5 50.6 reduce-scatter.2
  302.7 37.3 reduce-scatter.4

commit v7 on v5

--- a/solution.py
+++ b/solution.py
@@ -88,7 +88,7 @@
     act_proj = jnp.transpose(act_proj, (2, 0, 1, 3, 4)).reshape(2048, 256)
 
     piece = reduce(matmul(line, after(out_chip, act_line), 0), around)
-    grad_half = after(gather(piece, around).reshape(1024, 896), act_proj)
+    grad_half = gather(after(piece, act_proj), around).reshape(1024, 896)
     grad_proj = jnp.concatenate([grad_half, swap(grad_half)], 0)
 
     act_square = act_proj * act_proj

time: 379 us -> 374 us (0.987)
  local copies, waits for them, and re-layouts: 17 us -> 12.5 us
    all_to_all x3 -> x2, blocking collectives: 82 us -> 52 us  [reduce(): got = lax.all_to_all(value, axes, 0, 0, tiled=True)]
    all_to_all x3 -> x4, blocking collectives: 78.3 us -> 105 us  [gather(): return lax.all_to_all(copies, axes, 0, 0, tiled=True)]
    all_to_all x2 -> x3, starting transfers between devices: 13.5 us -> 18.4 us  [reduce(): got = lax.all_to_all(value, axes, 0, 0, tiled=True)]
    all_to_all x3 -> x2, starting transfers between devices: 15.5 us -> 11.2 us  [gather(): return lax.all_to_all(copies, axes, 0, 0, tiled=True)]
    unnamed x30 -> x31, local copies, waits for them, and re-layouts: 8.9 us -> 5.86 us
    all_to_all x2 -> x3, waiting for transfers between devices: 17.7 us -> 17.5 us  [reduce(): got = lax.all_to_all(value, axes, 0, 0, tiled=True)]
    all_to_all x3 -> x2, waiting for transfers between devices: 20.7 us -> 20.7 us  [gather(): return lax.all_to_all(copies, axes, 0, 0, tiled=True)]
  transfers between devices with their start and end apart: 15 -> 15, of which waited for: 10 -> 11; matrix products, arithmetic and copies ran while one was open for 5% -> 4% of each run, Pallas kernels for 1% -> 1%
where the time goes in v7:
time: 374 us; the launch traced here: 373 us
  blocking collectives  157 us (42%)
  waiting for transfers between devices  119 us (32%)
  starting transfers between devices  38.6 us (10%)
  Pallas kernels  15.4 us (4%)
  between operations  14.1 us (4%)
  local copies, waits for them, and re-layouts  12.5 us (3%)
  other arithmetic  10.1 us (3%)
  matrix products  5.57 us (1%)
    all_to_all x4, blocking collectives, gather(): return lax.all_to_all(copies, axes, 0, 0, tiled=True)  105 us
    all_to_all x2, blocking collectives, reduce(): got = lax.all_to_all(value, axes, 0, 0, tiled=True)  52 us
    reduce_scatter x2, waiting for transfers between devices, body(): update = lax.psum_scatter(update, 'x', scatter_dimension=0, tiled=True)  37.8 us
    all_gather x1, waiting for transfers between devices, body(): lax.all_gather(act_line.reshape(512, 256), 'x', axis=0)  28.2 us
    all_to_all x2, waiting for transfers between devices, gather(): return lax.all_to_all(copies, axes, 0, 0, tiled=True)  20.7 us
    all_to_all x3, starting transfers between devices, reduce(): got = lax.all_to_all(value, axes, 0, 0, tiled=True)  18.4 us
    all_to_all x3, waiting for transfers between devices, reduce(): got = lax.all_to_all(value, axes, 0, 0, tiled=True)  17.5 us
    pallas_call x3, Pallas kernels, matmul(): pl.pallas_call(kernel, out_shape=jax.ShapeDtypeStruct((rows, columns), bf...  15.4 us
  transfers between devices with their start and end apart: 15, of which 11 were waited for; matrix products, arithmetic and copies ran while one was open for 4% of the time, Pallas kernels for 1%

profile of v7, /device:TPU:1, one launch (start us, length us, event | category | flops | bytes accessed | tf_op | source)
XLA Modules:
  0.0 372.9 jit_solution(4449512360989401025)
XLA Ops:
  8.3 3.3 collective-permute-start
  12.7 29.2 %all_to_all.75 = bf16[4,64,1792]{2,1,0:T(8,128)(2,1)} all-to-all(bf16[4,64,1792]{2,1,0:T(8,128)(2,1)S(1)} %broadcast_in_dim.12), channel_id=1, replica_groups=mesh['x'=4,'zh'=4,'y'=4,'zl'=2,'c'=2] {'zh'}, dimensions={0} | all-to-all | bytes 1835008 | tf_op jit(solution)/shard_map/all_to_all | solution.py:64
  43.0 7.8 %all-to-all-start.1 = ((bf16[16,128,256]{2,1,0:T(8,128)(2,1)}), bf16[16,128,256]{2,1,0:T(8,128)(2,1)S(1)}, u32[]{:S(2)}, u32[]{:S(2)}) async-start(bf16[16,128,256]{2,1,0:T(8,128)(2,1)} %broadcast_in_dim.13), calls=%async_computation.1 | async-start | bytes 2097152 | tf_op jit(solution)/shard_map/all_to_all | solution.py:64
  51.0 15.6 %all-to-all-done.1 = bf16[16,128,256]{2,1,0:T(8,128)(2,1)S(1)} async-done(((bf16[16,128,256]{2,1,0:T(8,128)(2,1)}), bf16[16,128,256]{2,1,0:T(8,128)(2,1)S(1)}, u32[]{:S(2)}, u32[]{:S(2)}) %all-to-all-start.1) | async-done | bytes 1048608 | tf_op jit(solution)/shard_map/all_to_all | solution.py:64
  67.8 3.4 all-to-all-start.2
  71.2 1.6 constant_dynamic-update-slice_fusion.1
  72.8 1.7 constant_dynamic-update-slice_fusion.b_ref
  74.5 5.1 %all-to-all-done.2 = bf16[4,2,64,256]{3,2,1,0:T(8,128)(2,1)S(1)} async-done(((bf16[4,2,64,256]{3,2,1,0:T(8,128)(2,1)}), bf16[4,2,64,256]{3,2,1,0:T(8,128)(2,1)S(1)}, u32[]{:S(2)}, u32[]{:S(2)}) %all-to-all-start.2) | async-done | bytes 262176 | tf_op jit(solution)/shard_map/all_to_all | solution.py:64
  79.6 8.7 %all-gather.5.cloned.1.call-done.a_ref = bf16[1024,1792]{1,0:T(8,128)(2,1)} async-done(((bf16[256,1792]{1,0:T(8,128)(2,1)}), bf16[1024,1792]{1,0:T(8,128)(2,1)}) %all-gather.5.cloned.1.call-update) | async-done | bytes 3670032 | tf_op jit(solution)/shard_map/all_gather | solution.py:83
  88.2 2.0 copy-done.1
  90.3 5.3 %shard_map.68 = bf16[1024,896]{1,0:T(8,128)(2,1)} custom-call(bf16[1024,1792]{1,0:T(8,128)(2,1)S(1)} %copy-done.1, bf16[1792,896]{1,0:T(8,128)(2,1)S(1)} %constant_dynamic-update-slice_fusion.b_ref), custom_call_target="tpu_custom_call" | custom-call | flops 3288334336 | bytes 8716288 | tf_op jit(solution)/shard_map/pallas_call | solution.py:43
  95.5 5.0 %all-to-all-start.3 = ((bf16[8,128,896]{2,1,0:T(8,128)(2,1)}), bf16[8,128,896]{2,1,0:T(8,128)(2,1)}, u32[]{:S(2)}, u32[]{:S(2)}) async-start(bf16[8,128,896]{2,1,0:T(8,128)(2,1)} %bitcast.11), calls=%async_computation.3 | async-start | bytes 3670016 | tf_op jit(solution)/shard_map/all_to_all | solution.py:68
  101.3 28.2 %all-gather.3.cloned.1.call-done = bf16[4,512,256]{2,1,0:T(8,128)(2,1)} async-done(((bf16[1,512,256]{2,1,0:T(8,128)(2,1)}), bf16[4,512,256]{2,1,0:T(8,128)(2,1)}) %all-gather.3.cloned.1.call-update) | async-done | bytes 1048592 | tf_op jit(solution)/shard_map/all_gather | solution.py:87
  129.6 2.3 copy.11
  131.9 1.8 reduce_sum.54
  133.9 27.2 %all_to_all.76 = bf16[8,128,896]{2,1,0:T(8,128)(2,1)S(1)} all-to-all(bf16[8,128,896]{2,1,0:T(8,128)(2,1)S(1)} %broadcast_in_dim.15), channel_id=1, replica_groups=mesh['x'=4,'zh'=4,'y'=4,'zl'=2,'c'=2] {'y','zl'}, dimensions={0} | all-to-all | bytes 3670016 | tf_op jit(solution)/shard_map/all_to_all | solution.py:64
  161.2 2.8 collective-permute-start.2
  165.0 2.3 collective-permute-done.2
  173.5 31.7 %all_to_all.77 = bf16[8,160,896]{2,1,0:T(8,128)(2,1)} all-to-all(bf16[8,160,896]{2,1,0:T(8,128)(2,1)S(1)} %bitcast.49), channel_id=1, replica_groups=mesh['x'=4,'zh'=4,'y'=4,'zl'=2,'c'=2] {'y','zl'}, dimensions={0} | all-to-all | bytes 4587520 | tf_op jit(solution)/shard_map/all_to_all | solution.py:68
  205.2 2.0 reduce_sum.55
  207.4 30.6 %all_to_all.78 = bf16[8,160,896]{2,1,0:T(8,128)(2,1)S(1)} all-to-all(bf16[8,160,896]{2,1,0:T(8,128)(2,1)S(1)} %broadcast_in_dim.16), channel_id=1, replica_groups=mesh['x'=4,'zh'=4,'y'=4,'zl'=2,'c'=2] {'y','zl'}, dimensions={0} | all-to-all | bytes 4587520 | tf_op jit(solution)/shard_map/all_to_all | solution.py:64
  237.9 5.7 %shard_map.69 = bf16[1280,1792]{1,0:T(8,128)(2,1)S(1)} custom-call(bf16[1280,896]{1,0:T(8,128)(2,1)S(1)} %bitcast.44, bf16[1792,896]{1,0:T(8,128)(2,1)S(1)} %constant_dynamic-update-slice_fusion.b_ref), custom_call_target="tpu_custom_call" | custom-call | flops 4110417920 | bytes 10092544 | tf_op jit(solution)/shard_map/pallas_call | solution.py:43
  243.7 2.1 copy-done
  248.3 20.3 %all_to_all.79 = bf16[8,96,896]{2,1,0:T(8,128)(2,1)} all-to-all(bf16[8,96,896]{2,1,0:T(8,128)(2,1)S(1)} %bitcast.53), channel_id=1, replica_groups=mesh['x'=4,'zh'=4,'y'=4,'zl'=2,'c'=2] {'y','zl'}, dimensions={0} | all-to-all | bytes 2752512 | tf_op jit(solution)/shard_map/all_to_all | solution.py:68
  270.3 18.4 %all_to_all.80 = bf16[8,96,896]{2,1,0:T(8,128)(2,1)S(1)} all-to-all(bf16[8,96,896]{2,1,0:T(8,128)(2,1)S(1)} %broadcast_in_dim.17), channel_id=1, replica_groups=mesh['x'=4,'zh'=4,'y'=4,'zl'=2,'c'=2] {'y','zl'}, dimensions={0} | all-to-all | bytes 2752512 | tf_op jit(solution)/shard_map/all_to_all | solution.py:64
  288.7 4.4 %shard_map.70 = bf16[768,1792]{1,0:T(8,128)(2,1)} custom-call(bf16[768,896]{1,0:T(8,128)(2,1)S(1)} %bitcast.45, bf16[1792,896]{1,0:T(8,128)(2,1)S(1)} %constant_dynamic-update-slice_fusion.b_ref), custom_call_target="tpu_custom_call" | custom-call | flops 2466250752 | bytes 7340032 | tf_op jit(solution)/shard_map/pallas_call | solution.py:43
  293.1 4.7 %reduce-scatter.3.cloned.1.call-done = bf16[320,1792]{1,0:T(8,128)(2,1)} async-done(((bf16[1280,1792]{1,0:T(8,128)(2,1)}), bf16[320,1792]{1,0:T(8,128)(2,1)}) %reduce-scatter.3.cloned.1.call-update) | async-done | bytes 1146896 | tf_op jit(solution)/shard_map/reduce_scatter | solution.py:114
  297.8 6.7 %all-to-all-start.7 = ((bf16[4,80,1792]{2,1,0:T(8,128)(2,1)}), bf16[4,80,1792]{2,1,0:T(8,128)(2,1)S(1)}, u32[]{:S(2)}, u32[]{:S(2)}) async-start(bf16[4,80,1792]{2,1,0:T(8,128)(2,1)} %bitcast.55), calls=%async_computation.8 | async-start | bytes 2293760 | tf_op jit(solution)/shard_map/all_to_all | solution.py:68
  304.5 33.1 %reduce-scatter.5.cloned.1.call-done = bf16[192,1792]{1,0:T(8,128)(2,1)} async-done(((bf16[768,1792]{1,0:T(8,128)(2,1)}), bf16[192,1792]{1,0:T(8,128)(2,1)}) %reduce-scatter.5.cloned.1.call-update) | async-done | bytes 688144 | tf_op jit(solution)/shard_map/reduce_scatter | solution.py:114
  337.6 6.7 %all-to-all-start.10 = ((bf16[4,48,1792]{2,1,0:T(8,128)(2,1)}), bf16[4,48,1792]{2,1,0:T(8,128)(2,1)S(1)}, u32[]{:S(2)}, u32[]{:S(2)}) async-start(bf16[4,48,1792]{2,1,0:T(8,128)(2,1)} %bitcast.61), calls=%async_computation.12 | async-start | bytes 1376256 | tf_op jit(solution)/shard_map/all_to_all | solution.py:68
  344.5 17.5 %all-to-all-done.10 = bf16[4,48,1792]{2,1,0:T(8,128)(2,1)S(1)} async-done(((bf16[4,48,1792]{2,1,0:T(8,128)(2,1)}), bf16[4,48,1792]{2,1,0:T(8,128)(2,1)S(1)}, u32[]{:S(2)}, u32[]{:S(2)}) %all-to-all-start.10) | async-done | bytes 688160 | tf_op jit(solution)/shard_map/all_to_all | solution.py:68
  362.2 2.0 collective-permute-start.5
  (72 shorter events, 19.7 us)
Async XLA Ops:
  7.2 81.1 %all-gather.5.cloned.1.call-start = ((), (), s32[]{:S(2)}) async-start(), calls=%async_computation.14 | async-start | bytes 4587520 | tf_op jit(solution)/shard_map/all_gather | solution.py:83
  8.3 4.3 %collective-permute-start = (bf16[64,896]{1,0:T(8,128)(2,1)S(1)}, bf16[64,896]{1,0:T(8,128)(2,1)S(1)}, u32[]{:S(2)}, u32[]{:S(2)}) collective-permute-start(bf16[64,896]{1,0:T(8,128)(2,1)S(1)} %get-tuple-element.15), channel_id=1, source_target_pairs={{0,1},{1,0},{2,3},{3,2},{4,5},{5,4},{6,7},{7,6},{8,9},{9,8},{10,11... | collective-permute-start | bytes 344072 | tf_op jit(solution)/shard_map/ppermute | solution.py:18
  12.6 29.3 %copy-start.12 = (bf16[128,256]{1,0:T(8,128)(2,1)S(1)}, bf16[128,256]{1,0:T(8,128)(2,1)}, u32[]{:S(2)}) copy-start(bf16[128,256]{1,0:T(8,128)(2,1)} %param.5) | copy-start | bytes 196612
  41.9 24.7 %copy-start.3 = (bf16[4096,256]{1,0:T(8,128)(2,1)S(1)}, bf16[4096,256]{1,0:T(8,128)(2,1)}, u32[]{:S(2)}) copy-start(bf16[4096,256]{1,0:T(8,128)(2,1)} %param.7) | copy-start | bytes 6291460
  43.0 23.6 %all-to-all-start.1 = ((bf16[16,128,256]{2,1,0:T(8,128)(2,1)}), bf16[16,128,256]{2,1,0:T(8,128)(2,1)S(1)}, u32[]{:S(2)}, u32[]{:S(2)}) async-start(bf16[16,128,256]{2,1,0:T(8,128)(2,1)} %broadcast_in_dim.13), calls=%async_computation.1 | async-start | bytes 2097152 | tf_op jit(solution)/shard_map/all_to_all | solution.py:64
  50.8 22.1 %collective-permute-start.1 = (bf16[896,896]{1,0:T(8,128)(2,1)}, bf16[896,896]{1,0:T(8,128)(2,1)}, u32[]{:S(2)}, u32[]{:S(2)}) collective-permute-start(bf16[896,896]{1,0:T(8,128)(2,1)} %param.8), channel_id=1, source_target_pairs={{0,1},{1,0},{2,3},{3,2},{4,5},{5,4},{6,7},{7,6},{8,9},{9,8},{10,11... | collective-permute-start | bytes 4816904 | tf_op jit(solution)/shard_map/ppermute | solution.py:18
  67.8 11.8 %all-to-all-start.2 = ((bf16[4,2,64,256]{3,2,1,0:T(8,128)(2,1)}), bf16[4,2,64,256]{3,2,1,0:T(8,128)(2,1)S(1)}, u32[]{:S(2)}, u32[]{:S(2)}) async-start(bf16[4,2,64,256]{3,2,1,0:T(8,128)(2,1)} %broadcast_in_dim.14), calls=%async_computation.2 | async-start | bytes 524288 | tf_op jit(solution)/shard_map/all_to_all | solution.py:64
  79.6 16.0 %copy-start.7 = (bf16[4,2,64,256]{3,2,1,0:T(8,128)(2,1)}, bf16[4,2,64,256]{3,2,1,0:T(8,128)(2,1)S(1)}, u32[]{:S(2)}) copy-start(bf16[4,2,64,256]{3,2,1,0:T(8,128)(2,1)S(1)} %all-to-all-done.2) | copy-start | bytes 786436
  88.2 2.0 copy-start.1
  95.5 36.3 %all-to-all-start.3 = ((bf16[8,128,896]{2,1,0:T(8,128)(2,1)}), bf16[8,128,896]{2,1,0:T(8,128)(2,1)}, u32[]{:S(2)}, u32[]{:S(2)}) async-start(bf16[8,128,896]{2,1,0:T(8,128)(2,1)} %bitcast.11), calls=%async_computation.3 | async-start | bytes 3670016 | tf_op jit(solution)/shard_map/all_to_all | solution.py:68
  100.5 29.0 %all-gather.3.cloned.1.call-start = ((), (), s32[]{:S(2)}) async-start(), calls=%async_computation.13 | async-start | bytes 1310720 | tf_op jit(solution)/shard_map/all_gather | solution.py:87
  101.3 196.5 %reduce-scatter.3.cloned.1.call-start = ((), (), s32[]{:S(2)}) async-start(), calls=%async_computation.15 | async-start | bytes 5734400 | tf_op jit(solution)/shard_map/reduce_scatter | solution.py:114
  133.9 30.0 %copy-start.4 = (bf16[4096,256]{1,0:T(8,128)(2,1)S(1)}, bf16[4096,256]{1,0:T(8,128)(2,1)}, u32[]{:S(2)}) copy-start(bf16[4096,256]{1,0:T(8,128)(2,1)} %param.7) | copy-start | bytes 6291460
  161.2 6.2 %collective-permute-start.2 = (bf16[1024,896]{1,0:T(8,128)(2,1)S(1)}, bf16[1024,896]{1,0:T(8,128)(2,1)S(1)}, u32[]{:S(2)}, u32[]{:S(2)}) collective-permute-start(bf16[1024,896]{1,0:T(8,128)(2,1)S(1)} %bitcast.50), channel_id=1, source_target_pairs={{0,1},{1,0},{2,3},{3,2},{4,5},{5,4},{6,7},{7,6},{8,9},{9,8},{10,11... | collective-permute-start | bytes 5505032 | tf_op jit(solution)/shard_map/ppermute | solution.py:18
  164.7 2.7 copy-start.6
  164.7 2.7 copy-start.13
  164.9 5.5 %copy-start.2 = (bf16[16,128,256]{2,1,0:T(8,128)(2,1)}, bf16[16,128,256]{2,1,0:T(8,128)(2,1)S(1)}, u32[]{:S(2)}) copy-start(bf16[16,128,256]{2,1,0:T(8,128)(2,1)S(1)} %get-tuple-element.10) | copy-start | bytes 3145732
  164.9 5.5 %collective-permute-start.3 = (bf16[16,128,256]{2,1,0:T(8,128)(2,1)S(1)}, bf16[16,128,256]{2,1,0:T(8,128)(2,1)S(1)}, u32[]{:S(2)}, u32[]{:S(2)}) collective-permute-start(bf16[16,128,256]{2,1,0:T(8,128)(2,1)S(1)} %get-tuple-element.11), channel_id=1, source_target_pairs={{0,1},{1,0},{2,3},{3,2},{4,5},{5,4},{6,7},{7,6},{8,9},{9,8},{10,11... | collective-permute-start | bytes 3145736 | tf_op jit(solution)/shard_map/ppermute | solution.py:18
  168.7 1.3 copy-start.14
  170.0 3.5 copy-start.8
  170.0 1.9 collective-permute-start.4
  170.5 3.0 copy-start.5
  171.9 1.6 copy-start.10
  243.7 2.1 copy-start
  245.8 91.8 %reduce-scatter.5.cloned.1.call-start = ((), (), s32[]{:S(2)}) async-start(), calls=%async_computation.16 | async-start | bytes 3440640 | tf_op jit(solution)/shard_map/reduce_scatter | solution.py:114
  245.9 1.3 copy-start.9
  245.9 1.4 copy-start.11
  297.8 39.8 %all-to-all-start.7 = ((bf16[4,80,1792]{2,1,0:T(8,128)(2,1)}), bf16[4,80,1792]{2,1,0:T(8,128)(2,1)S(1)}, u32[]{:S(2)}, u32[]{:S(2)}) async-start(bf16[4,80,1792]{2,1,0:T(8,128)(2,1)} %bitcast.55), calls=%async_computation.8 | async-start | bytes 2293760 | tf_op jit(solution)/shard_map/all_to_all | solution.py:68
  337.6 24.4 %all-to-all-start.10 = ((bf16[4,48,1792]{2,1,0:T(8,128)(2,1)}), bf16[4,48,1792]{2,1,0:T(8,128)(2,1)S(1)}, u32[]{:S(2)}, u32[]{:S(2)}) async-start(bf16[4,48,1792]{2,1,0:T(8,128)(2,1)} %bitcast.61), calls=%async_computation.12 | async-start | bytes 1376256 | tf_op jit(solution)/shard_map/all_to_all | solution.py:68
  362.2 3.1 collective-permute-start.5
Sparse Core Ops, SparseCore 0:
  42.0 46.1 all-gather.4
  103.8 25.7 all-gather.2
  245.9 51.8 reduce-scatter.2
  300.2 37.3 reduce-scatter.4
